TPU v7x, 32 devices: a whole 2x2x4 slice. The times are simulated.
32 devices in a mesh: dp: 8 (over z, core), heads: 2 (over x), expert: 2 (over y).
Axes of the slice: x: 2, y: 2, z: 4, core: 2. Of those that a mesh axis runs over, the one named last changes fastest.
Arguments:
- block_in: bfloat16 [64, 197, 768], P(('dp', 'expert'), None, 'heads'), may hold values from -6 to 6
- cotangent: bfloat16 [64, 197, 768], P(('dp', 'expert'), None, 'heads'), may hold values from -8 to 8
- route_ids: int32 [64, 197, 2], P(('dp', 'expert')), may hold values from 0 to 7, all different within a row; in each aligned block of 788 rows (0 to 787, 788 to 1575, ..., all dimensions but the last counted through in order) at most 281 rows name the same one
- gain_attn: bfloat16 [768], P(('dp', 'expert')), may hold values from 0.099609375 to 1.8984375
- w_qkv: bfloat16 [768, 3, 768], P(('dp', 'expert'), None, 'heads'), may hold values from -0.21875 to 0.21875
- w_out_attn: bfloat16 [768, 768], P(('dp', 'expert'), 'heads'), may hold values from -0.875 to 0.875
- gain_moe: bfloat16 [768], P(('dp', 'expert')), may hold values from 0.099609375 to 1.8984375
- router: bfloat16 [768, 8], P(('dp', 'expert')), may hold values from -0.21875 to 0.21875
- w_in: bfloat16 [768, 8, 3072], P('dp', 'expert', 'heads'), may hold values from -0.21875 to 0.21875
- w_out: bfloat16 [768, 8, 3072], P('dp', 'expert', 'heads'), may hold values from -2.5 to 2.5
Outputs:
- block_out: bfloat16 [64, 197, 768], P(('dp', 'expert'), None, 'heads')
- grad_block_in: bfloat16 [64, 197, 768], P(('dp', 'expert'), None, 'heads')
- grad_gain_attn: float32 [768], P(('dp', 'expert'))
- grad_w_qkv: float32 [768, 3, 768], P(('dp', 'expert'), None, 'heads')
- grad_w_out_attn: float32 [768, 768], P(('dp', 'expert'), 'heads')
- grad_gain_moe: float32 [768], P(('dp', 'expert'))
- grad_router: float32 [768, 8], P(('dp', 'expert'))
- grad_w_in: float32 [768, 8, 3072], P('dp', 'expert', 'heads')
- grad_w_out: float32 [768, 8, 3072], P('dp', 'expert', 'heads')
Inputs may be any that keep to these rules, and one draw needn't show every extreme that they name: `route_ids`: each token names two different experts. Within each aligned block of 788 tokens (the images of one index of dp and expert) no expert is named more than 281 times, a bound that some block reaches.
All inputs are finite; a program needn't handle non-finite values.
Results may differ from a plain program's by a relative error of at most 0.022.
Values may be sent and summed in bfloat16 or wider, within the bound.
No kernel may reach another device: no remote copies, remote signals or barrier semaphores. Data moves between devices by JAX's collectives and lax.ppermute only.
A program may use at most 192 MiB of HBM per device.

v0:
```python
import jax
import jax.numpy as jnp
from jax import lax
from jax.sharding import PartitionSpec as P

HEAD_DIM = 64


def layer_norm(inputs, norm_gain):
    average = jnp.mean(inputs, axis=-1, keepdims=True)
    centred = inputs - average
    spread = jnp.mean(centred * centred, axis=-1, keepdims=True)
    return centred * lax.rsqrt(spread + 1e-06) * norm_gain


def per_device(
    block_in, cotangent, route_ids, gain_attn, w_qkv, w_out_attn, gain_moe, router, w_in, w_out
):
    full_in, full_grad = (
        lax.all_gather(block_in, "heads", axis=2, tiled=True),
        lax.all_gather(cotangent, "heads", axis=2, tiled=True),
    )
    gain_one, qkv_weight, out_weight, gain_two, router_weight = (
        lax.all_gather(gain_attn, ("dp", "expert"), axis=0, tiled=True),
        lax.all_gather(w_qkv, ("dp", "expert"), axis=0, tiled=True),
        lax.all_gather(w_out_attn, ("dp", "expert"), axis=0, tiled=True),
        lax.all_gather(gain_moe, ("dp", "expert"), axis=0, tiled=True),
        lax.all_gather(router, ("dp", "expert"), axis=0, tiled=True),
    )
    expert_in, expert_out = (
        lax.all_gather(w_in, "dp", axis=0, tiled=True),
        lax.all_gather(w_out, "dp", axis=0, tiled=True),
    )
    images, seq_len, model_width = full_in.shape
    token_count = images * seq_len
    inputs = full_in.reshape(token_count, model_width).astype(jnp.float32)
    gain_first = gain_one.astype(jnp.float32)
    gain_second = gain_two.astype(jnp.float32)
    head_index = lax.axis_index("heads")
    half_width = model_width // lax.axis_size("heads")
    normed_one = layer_norm(inputs, gain_first).astype(jnp.bfloat16)
    projected = jnp.einsum(
        "td,dkh->tkh", normed_one, qkv_weight, preferred_element_type=jnp.float32
    ).astype(jnp.bfloat16)
    local_width = projected.shape[2]
    local_heads = local_width // HEAD_DIM
    head_parts = projected.reshape(images, seq_len, 3, local_heads, HEAD_DIM)
    queries = head_parts[:, :, 0]
    keys_in = head_parts[:, :, 1]
    values_in = head_parts[:, :, 2]
    score_scale = HEAD_DIM ** (-0.5)
    scores = (
        jnp.einsum("iqhc,ikhc->ihqk", queries, keys_in, preferred_element_type=jnp.float32)
        * score_scale
    )
    row_top = jnp.max(scores, axis=-1, keepdims=True)
    log_total = row_top + jnp.log(jnp.sum(jnp.exp(scores - row_top), axis=-1, keepdims=True))
    weights = jnp.exp(scores - log_total).astype(jnp.bfloat16)
    context = (
        jnp.einsum("ihqk,ikhc->iqhc", weights, values_in, preferred_element_type=jnp.float32)
        .astype(jnp.bfloat16)
        .reshape(token_count, local_width)
    )
    attn_part = jnp.einsum("th,dh->td", context, out_weight, preferred_element_type=jnp.float32)
    middle = inputs + lax.psum(attn_part, "heads")
    normed_two = layer_norm(middle, gain_second).astype(jnp.bfloat16)
    logits = jnp.dot(normed_two, router_weight, preferred_element_type=jnp.float32)
    route_probs = jax.nn.softmax(logits, axis=-1)
    expert_count = router_weight.shape[1]
    capacity = 20 * token_count // (7 * expert_count)
    pair_ids = route_ids.reshape(token_count * 2)
    one_hot = (pair_ids[:, None] == jnp.arange(expert_count, dtype=jnp.int32)[None, :]).astype(
        jnp.int32
    )
    slot_rank = jnp.sum((jnp.cumsum(one_hot, axis=0) - one_hot) * one_hot, axis=1)
    flat_index = pair_ids * capacity + slot_rank
    pair_range = jnp.arange(token_count * 2, dtype=jnp.int32)
    slot_owner = jnp.zeros(expert_count * capacity, jnp.int32).at[flat_index].set(pair_range)
    filled = jnp.zeros(expert_count * capacity, jnp.int32).at[flat_index].set(1) > 0
    source_rows = slot_owner // 2
    choice_mask = one_hot.reshape(token_count, 2, expert_count).astype(jnp.float32)
    gate_values = jnp.sum(choice_mask * route_probs[:, None, :], axis=2)
    send_rows = jnp.where(
        filled[:, None], normed_two[source_rows], jnp.zeros((), jnp.bfloat16)
    ).reshape(expert_count, capacity, model_width)
    received = lax.all_to_all(send_rows, "expert", split_axis=0, concat_axis=1, tiled=True)
    hidden = jnp.einsum("erd,def->erf", received, expert_in, preferred_element_type=jnp.float32)
    active = jax.nn.gelu(hidden).astype(jnp.bfloat16)
    expert_part = jnp.einsum("erf,def->erd", active, expert_out, preferred_element_type=jnp.float32)
    expert_result = lax.psum_scatter(
        expert_part.astype(jnp.bfloat16), "heads", scatter_dimension=2, tiled=True
    )
    result_width = expert_result.shape[2]
    returned = lax.all_to_all(
        expert_result, "expert", split_axis=1, concat_axis=0, tiled=True
    ).reshape(expert_count * capacity, result_width)
    picked = returned[flat_index].reshape(token_count, 2, result_width).astype(jnp.float32)
    grad_out = full_grad.reshape(token_count, model_width).astype(jnp.float32)
    middle_own = lax.dynamic_slice_in_dim(middle, head_index * half_width, half_width, 1)
    grad_own = lax.dynamic_slice_in_dim(grad_out, head_index * half_width, half_width, 1)
    block_own = middle_own + jnp.sum(gate_values[:, :, None] * picked, axis=1)
    grad_gates = lax.psum(jnp.sum(grad_own[:, None, :] * picked, axis=2), "heads")
    gate_flat = gate_values.reshape(token_count * 2)
    grad_send = (
        jnp.where(filled[:, None], gate_flat[slot_owner][:, None] * grad_out[source_rows], 0.0)
        .astype(jnp.bfloat16)
        .reshape(expert_count, capacity, model_width)
    )
    grad_received = lax.all_to_all(grad_send, "expert", split_axis=0, concat_axis=1, tiled=True)
    hidden = jnp.einsum("erd,def->erf", received, expert_in, preferred_element_type=jnp.float32)
    active = jax.nn.gelu(hidden).astype(jnp.bfloat16)
    grad_active = jnp.einsum(
        "erd,def->erf", grad_received, expert_out, preferred_element_type=jnp.float32
    )
    grad_expert_out = jnp.einsum(
        "erd,erf->def", grad_received, active, preferred_element_type=jnp.float32
    )
    gelu_value, gelu_pull = jax.vjp(jax.nn.gelu, hidden)
    grad_hidden = gelu_pull(grad_active)[0].astype(jnp.bfloat16)
    grad_expert_in = jnp.einsum(
        "erd,erf->def", received, grad_hidden, preferred_element_type=jnp.float32
    )
    grad_rows_part = jnp.einsum(
        "erf,def->erd", grad_hidden, expert_in, preferred_element_type=jnp.float32
    )
    grad_rows = lax.psum_scatter(
        grad_rows_part.astype(jnp.bfloat16), "heads", scatter_dimension=2, tiled=True
    )
    rows_width = grad_rows.shape[2]
    grad_back = lax.all_to_all(
        grad_rows, "expert", split_axis=1, concat_axis=0, tiled=True
    ).reshape(expert_count * capacity, rows_width)
    back_rows = grad_back[flat_index].reshape(token_count, 2, rows_width).astype(jnp.float32)
    back_total = jnp.sum(back_rows, axis=1)
    back_total = lax.all_gather(
        back_total.astype(jnp.bfloat16), "heads", axis=1, tiled=True
    ).astype(back_total.dtype)
    grad_probs = jnp.sum(choice_mask * grad_gates[:, :, None], axis=1)
    grad_logits = (
        route_probs * (grad_probs - jnp.sum(grad_probs * route_probs, axis=1, keepdims=True))
    ).astype(jnp.bfloat16)
    grad_router = jnp.einsum(
        "td,te->de", normed_two, grad_logits, preferred_element_type=jnp.float32
    )
    grad_normed_two = (
        jnp.einsum("te,de->td", grad_logits, router_weight, preferred_element_type=jnp.float32)
        + back_total
    )
    second_value, second_pull = jax.vjp(layer_norm, middle, gain_second)
    grad_middle_norm, grad_gain_two = second_pull(grad_normed_two)
    grad_middle = grad_out + grad_middle_norm
    grad_attn = grad_middle.astype(jnp.bfloat16)
    grad_out_weight = jnp.einsum(
        "td,th->dh", grad_attn, context, preferred_element_type=jnp.float32
    )
    grad_context = (
        jnp.einsum("td,dh->th", grad_attn, out_weight, preferred_element_type=jnp.float32)
        .astype(jnp.bfloat16)
        .reshape(images, seq_len, local_heads, HEAD_DIM)
    )
    scores_again = (
        jnp.einsum("iqhc,ikhc->ihqk", queries, keys_in, preferred_element_type=jnp.float32)
        * score_scale
    )
    probs_again = jnp.exp(scores_again - log_total)
    grad_weights = jnp.einsum(
        "iqhc,ikhc->ihqk", grad_context, values_in, preferred_element_type=jnp.float32
    )
    grad_values = jnp.einsum(
        "ihqk,iqhc->ikhc",
        probs_again.astype(jnp.bfloat16),
        grad_context,
        preferred_element_type=jnp.float32,
    )
    grad_scores = (
        probs_again * (grad_weights - jnp.sum(grad_weights * probs_again, axis=-1, keepdims=True))
    ).astype(jnp.bfloat16)
    grad_queries = (
        jnp.einsum("ihqk,ikhc->iqhc", grad_scores, keys_in, preferred_element_type=jnp.float32)
        * score_scale
    )
    grad_keys = (
        jnp.einsum("ihqk,iqhc->ikhc", grad_scores, queries, preferred_element_type=jnp.float32)
        * score_scale
    )
    grad_projected = (
        jnp.stack((grad_queries, grad_keys, grad_values), axis=2)
        .astype(jnp.bfloat16)
        .reshape(token_count, 3, local_width)
    )
    grad_qkv_weight = jnp.einsum(
        "td,tkh->dkh", normed_one, grad_projected, preferred_element_type=jnp.float32
    )
    grad_normed_part = jnp.einsum(
        "tkh,dkh->td", grad_projected, qkv_weight, preferred_element_type=jnp.float32
    )
    grad_normed_one = lax.psum(grad_normed_part.astype(jnp.bfloat16), "heads").astype(jnp.float32)
    first_value, first_pull = jax.vjp(layer_norm, inputs, gain_first)
    grad_inputs_norm, grad_gain_one = first_pull(grad_normed_one)
    grad_inputs = grad_middle + grad_inputs_norm
    grad_inputs_own = lax.dynamic_slice_in_dim(grad_inputs, head_index * half_width, half_width, 1)
    block_grads = (
        lax.psum_scatter(grad_gain_one, ("dp", "expert"), scatter_dimension=0, tiled=True),
        lax.psum_scatter(grad_qkv_weight, ("dp", "expert"), scatter_dimension=0, tiled=True),
        lax.psum_scatter(grad_out_weight, ("dp", "expert"), scatter_dimension=0, tiled=True),
        lax.psum_scatter(grad_gain_two, ("dp", "expert"), scatter_dimension=0, tiled=True),
        lax.psum_scatter(grad_router, ("dp", "expert"), scatter_dimension=0, tiled=True),
    )
    expert_grads = (
        lax.psum_scatter(
            grad_expert_in.astype(jnp.bfloat16), "dp", scatter_dimension=0, tiled=True
        ).astype(jnp.float32),
        lax.psum_scatter(
            grad_expert_out.astype(jnp.bfloat16), "dp", scatter_dimension=0, tiled=True
        ).astype(jnp.float32),
    )
    out_rows = block_own.astype(jnp.bfloat16).reshape(images, seq_len, half_width)
    grad_rows_out = grad_inputs_own.astype(jnp.bfloat16).reshape(images, seq_len, half_width)
    return (
        out_rows,
        grad_rows_out,
        block_grads[0],
        block_grads[1],
        block_grads[2],
        block_grads[3],
        block_grads[4],
        expert_grads[0],
        expert_grads[1],
    )


def solution(mesh):
    return jax.shard_map(
        per_device,
        mesh=mesh,
        in_specs=(
            P(("dp", "expert"), None, "heads"),
            P(("dp", "expert"), None, "heads"),
            P(("dp", "expert"), None, None),
            P(("dp", "expert")),
            P(("dp", "expert"), None, "heads"),
            P(("dp", "expert"), "heads"),
            P(("dp", "expert")),
            P(("dp", "expert"), None),
            P("dp", "expert", "heads"),
            P("dp", "expert", "heads"),
        ),
        out_specs=(
            P(("dp", "expert"), None, "heads"),
            P(("dp", "expert"), None, "heads"),
            P(("dp", "expert")),
            P(("dp", "expert"), None, "heads"),
            P(("dp", "expert"), "heads"),
            P(("dp", "expert")),
            P(("dp", "expert"), None),
            P("dp", "expert", "heads"),
            P("dp", "expert", "heads"),
        ),
        check_vma=False,
    )
```

profile of v0, /device:TPU:0, one launch (start us, length us, event | category | flops | bytes accessed | tf_op | source)
XLA Modules:
  0.0 1246.5 jit_solution(1328850150708580334)
XLA Ops:
  13.1 34.9 %all-reduce.8 = (bf16[768]{0:T(1024)(128)(2,1)S(1)}, bf16[768]{0:T(1024)(128)(2,1)S(1)}) all-reduce(bf16[768]{0:T(1024)(128)(2,1)S(1)} %dynamic-update-slice, bf16[768]{0:T(1024)(128)(2,1)S(1)} %dynamic-update-slice.1), channel_id=1, replica_groups=mesh['dp'=8,'heads'=2,'expert'=2] {'dp','expert'}, use_global_device_ids=true, to_apply=%add.1 | all-reduce | flops 1536 | bytes 6144
  48.1 33.6 %all_gather.33 = bf16[768,384]{1,0:T(8,128)(2,1)S(1)} all-gather(bf16[48,384]{1,0:T(8,128)(2,1)} %param.15), channel_id=1, replica_groups=mesh['dp'=8,'heads'=2,'expert'=2] {'dp','expert'}, dimensions={0}, use_global_device_ids=true | all-gather | bytes 626688 | tf_op jit(solution)/shard_map/all_gather | solution.py:26
  128.4 30.9 %all-gather = bf16[16,48,8]{1,2,0:T(8,128)(2,1)S(1)} all-gather(bf16[1,48,8]{1,2,0:T(8,128)(2,1)S(1)} %bitcast.121), channel_id=1, replica_groups=mesh['dp'=8,'heads'=2,'expert'=2] {'dp','expert'}, dimensions={0}, use_global_device_ids=true | all-gather | bytes 13056 | tf_op jit(solution)/shard_map/all_gather | solution.py:28
  203.0 12.3 gather_fusion.2
  245.0 19.5 %all-to-all-done.2 = bf16[8,281,768]{2,1,0:T(8,128)(2,1)} async-done(((bf16[8,281,768]{2,1,0:T(8,128)(2,1)}), bf16[8,281,768]{2,1,0:T(8,128)(2,1)}, u32[]{:S(2)}, u32[]{:S(2)}) %all-to-all-start.2) | async-done | bytes 3452960 | tf_op jit(solution)/shard_map/all_to_all | solution.py:109
  278.8 29.1 %all-to-all-done = bf16[8,281,768]{2,1,0:T(8,128)(2,1)} async-done(((bf16[8,281,768]{2,1,0:T(8,128)(2,1)}), bf16[8,281,768]{2,1,0:T(8,128)(2,1)}, u32[]{:S(2)}, u32[]{:S(2)}) %all-to-all-start) | async-done | bytes 3452960 | tf_op jit(solution)/shard_map/all_to_all | solution.py:86
  316.5 12.3 fusion.55
  328.7 46.6 %all-gather.12.cloned.1.call-done = bf16[768,4,1536]{2,0,1:T(8,128)(2,1)} async-done(((bf16[96,4,1536]{2,0,1:T(8,128)(2,1)}), bf16[768,4,1536]{2,0,1:T(8,128)(2,1)}) %all-gather.12.cloned.1.call-update) | async-done | bytes 9437200 | tf_op jit(solution)/shard_map/all_gather | solution.py:31
  375.3 22.1 %fusion.6 = (bf16[4,562,1536]{2,1,0:T(8,128)(2,1)}, f32[4,562,1536]{2,1,0:T(8,128)}) fusion(f32[4,562,1536]{2,1,0:T(8,128)} %fusion.55, bf16[4,562,768]{2,1,0:T(8,128)(2,1)} %all_to_all.51, bf16[768,4,1536]{2,0,1:T(8,128)(2,1)} %all-gather.12.cloned.1.call-done), kind=kOutput, calls=%fused_computation.15 | convolution fusion | flops 5372755968 | bytes 47419392 | tf_op jit(solution)/shard_map/erd,def->erf/dot_general | solution.py:87
  397.4 13.5 %convolution_convert_fusion.1 = bf16[4,562,768]{2,1,0:T(8,128)(2,1)} fusion(bf16[768,4,1536]{2,0,1:T(8,128)(2,1)} %all-gather.14.cloned.1.call-done, f32[4,562,1536]{2,1,0:T(8,128)} %get-tuple-element.93), kind=kOutput, calls=%fused_computation.47 | convolution fusion | flops 5336500224 | bytes 26701824 | tf_op jit(solution)/shard_map/erf,def->erd/dot_general | solution.py:89
  426.5 12.3 convolution_convert_fusion
  454.0 18.7 %reduce-scatter.16.cloned.1.call-done = bf16[384,2248]{1,0:T(8,128)(2,1)} async-done(((bf16[768,2248]{1,0:T(8,128)(2,1)}), bf16[384,2248]{1,0:T(8,128)(2,1)}) %reduce-scatter.16.cloned.1.call-update) | async-done | bytes 1726480
  488.7 34.0 %reduce-scatter.18.cloned.1.call-done = bf16[384,2248]{1,0:T(8,128)(2,1)} async-done(((bf16[768,2248]{1,0:T(8,128)(2,1)}), bf16[384,2248]{1,0:T(8,128)(2,1)}) %reduce-scatter.18.cloned.1.call-update) | async-done | bytes 1726480
  537.5 16.3 %convert_bitcast_fusion = bf16[768,4,1536]{0,2,1:T(8,128)(2,1)} fusion(bf16[4,562,768]{2,1,0:T(8,128)(2,1)} %all_to_all.58, f32[4,562,1536]{2,1,0:T(8,128)} %get-tuple-element.93), kind=kOutput, calls=%fused_computation.17 | convolution fusion | flops 5339492352 | bytes 26701824 | tf_op jit(solution)/shard_map/erd,erf->def/dot_general | solution.py:115
  593.5 10.9 multiply_reduce_fusion.5
  604.4 21.5 %psum.22 = f32[788,2]{1,0:T(8,128)S(1)} all-reduce(f32[788,2]{1,0:T(8,128)S(1)} %get-tuple-element.67), channel_id=1, replica_groups=mesh['dp'=8,'heads'=2,'expert'=2] {'heads'}, use_global_device_ids=true, to_apply=%region_18.19 | all-reduce | flops 1576 | bytes 12608 | tf_op jit(solution)/shard_map/psum | solution.py:102
  628.9 13.3 %convert_bitcast_fusion.1 = bf16[768,4,1536]{0,2,1:T(8,128)(2,1)} fusion(bf16[4,562,1536]{2,1,0:T(8,128)(2,1)} %get-tuple-element.92, bf16[4,562,768]{2,1,0:T(8,128)(2,1)} %all_to_all.51), kind=kOutput, calls=%fused_computation.18 | convolution fusion | flops 5308416000 | bytes 19795968 | tf_op jit(solution)/shard_map/erd,erf->def/dot_general | solution.py:120
  642.2 16.7 %copy.248 = bf16[768,4,1536]{2,1,0:T(4,128)(2,1)} copy(bf16[768,4,1536]{0,2,1:T(8,128)(2,1)} %convert_bitcast_fusion.1) | data formatting | bytes 18874368 | tf_op jit(solution)/shard_map/convert_element_type | solution.py:211
  658.9 16.7 %copy.249 = bf16[768,4,1536]{2,1,0:T(4,128)(2,1)} copy(bf16[768,4,1536]{0,2,1:T(8,128)(2,1)} %convert_bitcast_fusion) | data formatting | bytes 18874368 | tf_op jit(solution)/shard_map/convert_element_type | solution.py:214
  735.7 323.7 %all-reduce.18.cloned.1.call-done = (bf16[768,4,1536]{2,1,0:T(4,128)(2,1)}, bf16[768,4,1536]{2,1,0:T(4,128)(2,1)}) async-done(((bf16[768,4,1536]{2,1,0:T(4,128)(2,1)}, bf16[768,4,1536]{2,1,0:T(4,128)(2,1)}), (bf16[768,4,1536]{2,1,0:T(4,128)(2,1)}, bf16[768,4,1536]{2,1,0:T(4,128)(2,1)})) %all-reduce.18.cloned.1.call-update) | async-done | bytes 18874384
  1064.1 41.5 %all-reduce.16.cloned.1.call-done = bf16[788,768]{1,0:T(8,128)(2,1)} async-done(((bf16[788,768]{1,0:T(8,128)(2,1)}), bf16[788,768]{1,0:T(8,128)(2,1)}) %all-reduce.16.cloned.1.call-update) | async-done | bytes 1210384 | tf_op jit(solution)/shard_map/psum | solution.py:197
  1111.3 33.8 %all-reduce.7 = (f32[768]{0:T(1024)S(1)}, f32[768]{0:T(1024)S(1)}) all-reduce(f32[768]{0:T(1024)S(1)} %get-tuple-element.65, f32[768]{0:T(1024)S(1)} %get-tuple-element.63), channel_id=4, replica_groups=mesh['dp'=8,'heads'=2,'expert'=2] {'dp','expert'}, use_global_device_ids=true, to_apply=%region_30.31.clone | all-reduce | flops 1536 | bytes 12288
  1146.2 21.9 %reduce-scatter.14.cloned.1.call-done = f32[48,384]{1,0:T(8,128)} async-done(((f32[768,384]{1,0:T(8,128)}), f32[48,384]{1,0:T(8,128)}) %reduce-scatter.14.cloned.1.call-update) | async-done | bytes 73744 | tf_op jit(solution)/shard_map/reduce_scatter | solution.py:205
  1168.2 71.3 %reduce-scatter.12.cloned.1.call-done = f32[48,3,384]{2,0,1:T(8,128)} async-done(((f32[768,3,384]{2,0,1:T(8,128)}), f32[48,3,384]{2,0,1:T(8,128)}) %reduce-scatter.12.cloned.1.call-update) | async-done | bytes 221200 | tf_op jit(solution)/shard_map/reduce_scatter | solution.py:204
  (299 shorter events, 321.6 us)
Async XLA Ops:
  7.2 74.5 %all-gather.8.cloned.1.call-start = ((), (), s32[]{:S(2)}) async-start(), calls=%async_computation.9 | async-start | bytes 1815552 | tf_op jit(solution)/shard_map/all_gather | solution.py:20
  7.9 85.1 %all-gather.10.cloned.1.call-start = ((), (), s32[]{:S(2)}) async-start(), calls=%async_computation.10 | async-start | bytes 1880064 | tf_op jit(solution)/shard_map/all_gather | solution.py:25
  8.7 168.7 %all-gather.16.cloned.1.call-start = ((), (), s32[]{:S(2)}) async-start(), calls=%async_computation.14 | async-start | bytes 1815552 | tf_op jit(solution)/shard_map/all_gather | solution.py:21
  9.4 187.4 %all-reduce.14.cloned.1.call-start = ((), (), s32[]{:S(2)}) async-start(), calls=%async_computation.11 | async-start | bytes 4866048 | tf_op jit(solution)/shard_map/psum | solution.py:65
  48.1 44.9 %copy-start.39 = (f32[768]{0:T(1024)}, f32[768]{0:T(1024)S(1)}, u32[]{:S(2)}) copy-start(f32[768]{0:T(1024)S(1)} %convert_element_type.130) | copy-start | bytes 9220
  81.7 37.6 %copy-start.19 = (bf16[768,384]{1,0:T(8,128)(2,1)}, bf16[768,384]{1,0:T(8,128)(2,1)S(1)}, u32[]{:S(2)}) copy-start(bf16[768,384]{1,0:T(8,128)(2,1)S(1)} %all_gather.33) | copy-start | bytes 1769476
  121.6 194.9 %all-gather.14.cloned.1.call-start = ((), (), s32[]{:S(2)}) async-start(), calls=%async_computation.13 | async-start | bytes 10616832 | tf_op jit(solution)/shard_map/all_gather | solution.py:32
  122.9 252.4 %all-gather.12.cloned.1.call-start = ((), (), s32[]{:S(2)}) async-start(), calls=%async_computation.12 | async-start | bytes 10616832 | tf_op jit(solution)/shard_map/all_gather | solution.py:31
  128.4 71.7 %copy-start.35 = (f32[768]{0:T(1024)}, f32[768]{0:T(1024)S(1)}, u32[]{:S(2)}) copy-start(f32[768]{0:T(1024)S(1)} %convert_element_type.138) | copy-start | bytes 9220
  159.4 41.0 %copy-start.30 = (bf16[768,8]{0,1:T(8,128)(2,1)}, bf16[768,8]{0,1:T(8,128)(2,1)S(1)}, u32[]{:S(2)}) copy-start(bf16[768,8]{0,1:T(8,128)(2,1)S(1)} %reshape.319) | copy-start | bytes 36868
  220.3 44.2 %all-to-all-start.2 = ((bf16[8,281,768]{2,1,0:T(8,128)(2,1)}), bf16[8,281,768]{2,1,0:T(8,128)(2,1)}, u32[]{:S(2)}, u32[]{:S(2)}) async-start(bf16[8,281,768]{2,1,0:T(8,128)(2,1)} %select_convert_fusion), calls=%async_computation.2 | async-start | bytes 7077888 | tf_op jit(solution)/shard_map/all_to_all | solution.py:109
  264.5 43.4 %all-to-all-start = ((bf16[8,281,768]{2,1,0:T(8,128)(2,1)}), bf16[8,281,768]{2,1,0:T(8,128)(2,1)}, u32[]{:S(2)}, u32[]{:S(2)}) async-start(bf16[8,281,768]{2,1,0:T(8,128)(2,1)} %broadcast_select_fusion), calls=%async_computation | async-start | bytes 7077888 | tf_op jit(solution)/shard_map/all_to_all | solution.py:86
  269.9 202.8 %reduce-scatter.16.cloned.1.call-start = ((), (), s32[]{:S(2)}) async-start(), calls=%async_computation.19 | async-start | bytes 5308416
  426.4 96.3 %reduce-scatter.18.cloned.1.call-start = ((), (), s32[]{:S(2)}) async-start(), calls=%async_computation.20 | async-start | bytes 5308416
  482.8 50.0 %all-to-all-start.1 = ((bf16[4,562,384]{2,0,1:T(4,128)(2,1)}), bf16[4,562,384]{2,0,1:T(4,128)(2,1)}, u32[]{:S(2)}, u32[]{:S(2)}) async-start(bf16[4,562,384]{2,0,1:T(4,128)(2,1)} %copy.226), calls=%async_computation.1 | async-start | bytes 3452928 | tf_op jit(solution)/shard_map/all_to_all | solution.py:94
  532.8 38.2 %all-to-all-start.3 = ((bf16[4,562,384]{2,0,1:T(4,128)(2,1)}), bf16[4,562,384]{2,0,1:T(4,128)(2,1)}, u32[]{:S(2)}, u32[]{:S(2)}) async-start(bf16[4,562,384]{2,0,1:T(4,128)(2,1)} %copy.233), calls=%async_computation.3 | async-start | bytes 3452928 | tf_op jit(solution)/shard_map/all_to_all | solution.py:130
  537.5 138.2 %all-gather.18.cloned.1.call-start = ((), (), s32[]{:S(2)}) async-start(), calls=%async_computation.15 | async-start | bytes 1824768 | tf_op jit(solution)/shard_map/all_gather | solution.py:135
  593.4 140.9 %reduce-scatter.20.cloned.1.call-start = ((), (), s32[]{:S(2)}) async-start(), calls=%async_computation.21 | async-start | bytes 417792
  628.8 430.6 %all-reduce.18.cloned.1.call-start = ((), (), s32[]{:S(2)}) async-start(), calls=%async_computation.22 | async-start | bytes 37748736
  675.6 430.0 %all-reduce.16.cloned.1.call-start = ((), (), s32[]{:S(2)}) async-start(), calls=%async_computation.16 | async-start | bytes 2433024 | tf_op jit(solution)/shard_map/psum | solution.py:197
  719.0 449.1 %reduce-scatter.14.cloned.1.call-start = ((), (), s32[]{:S(2)}) async-start(), calls=%async_computation.18 | async-start | bytes 1253376 | tf_op jit(solution)/shard_map/reduce_scatter | solution.py:205
  723.0 516.4 %reduce-scatter.12.cloned.1.call-start = ((), (), s32[]{:S(2)}) async-start(), calls=%async_computation.17 | async-start | bytes 3760128 | tf_op jit(solution)/shard_map/reduce_scatter | solution.py:204
  1059.4 46.1 %copy-start.7 = (f32[788,768]{1,0:T(8,128)S(1)}, f32[788,768]{1,0:T(8,128)}, u32[]{:S(2)}) copy-start(f32[788,768]{1,0:T(8,128)} %copy-done.5) | copy-start | bytes 7262212
  1064.1 44.0 %copy-start.48 = (f32[788]{0:T(1024)S(1)}, f32[788]{0:T(1024)}, u32[]{:S(2)}) copy-start(f32[788]{0:T(1024)} %copy-done.47) | copy-start | bytes 9460
  (48 other events, 135.2 us)
Sparse Core Ops, SparseCore 0:
  9.5 25.7 all-gather.7
  37.6 43.3 all-gather.9
  82.5 21.9 all-gather.15
  121.7 69.3 all-reduce.13
  193.1 90.8 all-gather.13
  286.1 89.1 all-gather.11
  426.5 46.0 reduce-scatter.15
  475.0 47.6 reduce-scatter.17
  593.6 30.8 all-gather.17
  628.9 55.5 reduce-scatter.19
  687.3 372.0 all-reduce.17
  1061.7 43.8 all-reduce.15
  1109.7 58.3 reduce-scatter.13
  1172.5 66.9 reduce-scatter.11
where the time goes:
time: 1260 us; the launch traced here: 1250 us
  waiting for transfers between devices  609 us (48%)
  local copies, waits for them, and re-layouts  265 us (21%)
  blocking collectives  155 us (12%)
  matrix products  130 us (10%)
  other arithmetic  49.2 us (4%)
  starting transfers between devices  21.2 us (2%)
  between operations  17.5 us (1%)
    unnamed x18, waiting for transfers between devices  379 us
    reduce_scatter x1, waiting for transfers between devices, per_device(): lax.psum_scatter(grad_qkv_weight, ('dp', 'expert'), scatter_dimension=0,...  71.3 us
    unnamed x2, blocking collectives  68.7 us
    unnamed x138, local copies, waits for them, and re-layouts  67.5 us
    all_gather x1, waiting for transfers between devices, per_device(): lax.all_gather(w_in, 'dp', axis=0, tiled=True)  46.6 us
    psum x1, waiting for transfers between devices, per_device(): lax.psum(grad_normed_part.astype(jnp.bfloat16), 'heads').astype(jnp.float32)  41.5 us
    all_gather x1, blocking collectives, per_device(): lax.all_gather(w_out_attn, ('dp', 'expert'), axis=0, tiled=True)  33.6 us
    all_gather x1, blocking collectives, per_device(): lax.all_gather(router, ('dp', 'expert'), axis=0, tiled=True)  30.9 us
  transfers between devices with their start and end apart: 18, of which 9 were waited for; matrix products, arithmetic and copies ran while one was open for 28% of the time, Pallas kernels for 0%

commit v1 on v0

v1 whole, which is shorter than its diff:
```python
import functools

import jax
import jax.numpy as jnp
from jax import lax
from jax.experimental import pallas as pl
from jax.experimental.pallas import tpu as pltpu
from jax.sharding import PartitionSpec as P

HEAD_DIM = 64
CORES = 2
EPS = 1e-06
F32 = jnp.float32
BF16 = jnp.bfloat16
VMEM_LIMIT = 56 * 1024 * 1024


def dot(a, b, ca, cb):
    return lax.dot_general(a, b, (((ca,), (cb,)), ((), ())), preferred_element_type=F32)


def params(dims):
    return pltpu.CompilerParams(
        dimension_semantics=("arbitrary",) * dims, vmem_limit_bytes=VMEM_LIMIT
    )


def norm_parts(rows):
    average = jnp.mean(rows, axis=-1, keepdims=True)
    centred = rows - average
    spread = jnp.mean(centred * centred, axis=-1, keepdims=True)
    scale = lax.rsqrt(spread + EPS)
    return centred * scale, scale


def attend_kernel(x_ref, gain_ref, wqkv_ref, wo_ref, part_ref, qkv_ref, ctx_ref):
    width = wo_ref.shape[1]
    unit, _ = norm_parts(x_ref[0].astype(F32))
    normed = (unit * gain_ref[...]).astype(BF16)
    for part in range(3):
        cols = slice(part * width, (part + 1) * width)
        qkv_ref[0, :, cols] = dot(normed, wqkv_ref[:, cols], 1, 0).astype(BF16)
    seq = x_ref.shape[1]
    lane = lax.broadcasted_iota(jnp.int32, (seq, 128), 1)
    for pair in range(width // 128):
        q, k, v = (
            qkv_ref[0, :, part * width + pair * 128 : part * width + (pair + 1) * 128]
            for part in range(3)
        )
        ctx = jnp.zeros((seq, 128), F32)
        for side in range(2):
            mine = (lane >= 64) if side else (lane < 64)
            own_k = jnp.where(mine, k, jnp.zeros_like(k))
            own_v = jnp.where(mine, v, jnp.zeros_like(v))
            scores = dot(q, own_k, 1, 1) * (HEAD_DIM**-0.5)
            powers = jnp.exp(scores - jnp.max(scores, axis=-1, keepdims=True))
            weights = powers / jnp.sum(powers, axis=-1, keepdims=True)
            ctx = ctx + dot(weights.astype(BF16), own_v, 1, 0)
        ctx_ref[0, :, pair * 128 : (pair + 1) * 128] = ctx.astype(BF16)
    part_ref[0] = dot(ctx_ref[0], wo_ref[...], 1, 1).astype(BF16)


def attend(inputs, gain, packed, width):
    images, seq, model = inputs.shape
    whole = lambda i: (i, 0, 0)
    return pl.pallas_call(
        attend_kernel,
        grid=(images,),
        in_specs=[
            pl.BlockSpec((1, seq, model), whole),
            pl.BlockSpec((1, model), lambda i: (0, 0)),
            pl.BlockSpec((model, 3 * width), lambda i: (0, 0)),
            pl.BlockSpec((model, width), lambda i: (0, 3)),
        ],
        out_specs=[
            pl.BlockSpec((1, seq, model), whole),
            pl.BlockSpec((1, seq, 3 * width), whole),
            pl.BlockSpec((1, seq, width), whole),
        ],
        out_shape=[
            jax.ShapeDtypeStruct((images, seq, model), BF16),
            jax.ShapeDtypeStruct((images, seq, 3 * width), BF16),
            jax.ShapeDtypeStruct((images, seq, width), BF16),
        ],
        compiler_params=params(1),
        cost_estimate=pl.CostEstimate(
            flops=2 * images * seq * model * width * 5,
            bytes_accessed=8 * images * seq * model,
            transcendentals=images * seq * seq * width // 64,
        ),
        name="attend",
    )(inputs, gain, packed, packed)


def attend_back_kernel(
    x_ref, gain_ref, datt_ref, qkv_ref, ctx_ref, wqkv_ref, wo_ref,
    dnorm_ref, stats_ref, dgain_ref, dwqkv_ref, dwo_ref, dproj_ref,
):
    width = wo_ref.shape[1]
    seq, model = x_ref.shape[1], x_ref.shape[2]

    @pl.when(pl.program_id(0) == 0)
    def _():
        dgain_ref[...] = jnp.zeros_like(dgain_ref)
        dwqkv_ref[...] = jnp.zeros_like(dwqkv_ref)
        dwo_ref[...] = jnp.zeros_like(dwo_ref)

    datt = datt_ref[0]
    dwo_ref[...] += dot(datt, ctx_ref[0], 0, 0)
    dctx_all = dot(datt, wo_ref[...], 1, 0).astype(BF16)
    lane = lax.broadcasted_iota(jnp.int32, (seq, 128), 1)
    for pair in range(width // 128):
        cols = slice(pair * 128, (pair + 1) * 128)
        q, k, v = (
            qkv_ref[0, :, part * width + pair * 128 : part * width + (pair + 1) * 128]
            for part in range(3)
        )
        dctx = dctx_all[:, cols]
        dq = jnp.zeros((seq, 128), F32)
        dk = jnp.zeros((seq, 128), F32)
        dv = jnp.zeros((seq, 128), F32)
        for side in range(2):
            mine = (lane >= 64) if side else (lane < 64)
            own = lambda t: jnp.where(mine, t, jnp.zeros_like(t))
            own_k, own_v = own(k), own(v)
            scores = dot(q, own_k, 1, 1) * (HEAD_DIM**-0.5)
            powers = jnp.exp(scores - jnp.max(scores, axis=-1, keepdims=True))
            weights = powers / jnp.sum(powers, axis=-1, keepdims=True)
            dweights = dot(dctx, own_v, 1, 1)
            inner = jnp.sum(dweights * weights, axis=-1, keepdims=True)
            dscores = (weights * (dweights - inner)).astype(BF16)
            dq = dq + dot(dscores, own_k, 1, 0)
            dk = dk + dot(dscores, own(q), 0, 0)
            dv = dv + dot(weights.astype(BF16), own(dctx), 0, 0)
        for part, value in enumerate((dq * HEAD_DIM**-0.5, dk * HEAD_DIM**-0.5, dv)):
            start = part * width + pair * 128
            dproj_ref[:, start : start + 128] = value.astype(BF16)
    dproj = dproj_ref[...]
    gain = gain_ref[...]
    unit, scale = norm_parts(x_ref[0].astype(F32))
    normed = (unit * gain).astype(BF16)
    dwqkv_ref[...] += dot(normed, dproj, 0, 0)
    dnormed = dot(dproj, wqkv_ref[...], 1, 1)
    dnorm_ref[0] = dnormed.astype(BF16)
    along = dnormed * unit
    dgain_ref[...] += jnp.sum(along, axis=0, keepdims=True)
    first = jnp.sum(dnormed * gain, axis=-1, keepdims=True)
    second = jnp.sum(along * gain, axis=-1, keepdims=True)
    stats_ref[0] = jnp.where(lane == 0, first, jnp.where(lane == 1, second, 0.0))


def attend_back(inputs, gain, datt, qkv, ctx, packed, width):
    images, seq, model = inputs.shape
    whole = lambda i: (i, 0, 0)
    fixed = lambda i: (0, 0)
    return pl.pallas_call(
        attend_back_kernel,
        grid=(images,),
        in_specs=[
            pl.BlockSpec((1, seq, model), whole),
            pl.BlockSpec((1, model), fixed),
            pl.BlockSpec((1, seq, model), whole),
            pl.BlockSpec((1, seq, 3 * width), whole),
            pl.BlockSpec((1, seq, width), whole),
            pl.BlockSpec((model, 3 * width), fixed),
            pl.BlockSpec((model, width), lambda i: (0, 3)),
        ],
        out_specs=[
            pl.BlockSpec((1, seq, model), whole),
            pl.BlockSpec((1, seq, 128), whole),
            pl.BlockSpec((1, model), fixed),
            pl.BlockSpec((model, 3 * width), fixed),
            pl.BlockSpec((model, width), fixed),
        ],
        out_shape=[
            jax.ShapeDtypeStruct((images, seq, model), BF16),
            jax.ShapeDtypeStruct((images, seq, 128), F32),
            jax.ShapeDtypeStruct((1, model), F32),
            jax.ShapeDtypeStruct((model, 3 * width), F32),
            jax.ShapeDtypeStruct((model, width), F32),
        ],
        scratch_shapes=[pltpu.VMEM((seq, 3 * width), BF16)],
        compiler_params=params(1),
        cost_estimate=pl.CostEstimate(
            flops=2 * images * seq * model * width * 14,
            bytes_accessed=16 * images * seq * model,
            transcendentals=images * seq * seq * width // 64,
        ),
        name="attend_back",
    )(inputs, gain, datt, qkv, ctx, packed, packed)


def expert_kernel(
    slot_ref, prob_ref, x_ref, grad_ref, win_ref, wout_ref,
    rows_ref, grows_ref, gact_ref, dhid_ref, dgate_ref, drows_ref, yrows_ref,
):
    slots = rows_ref.shape[2]
    tokens, model = x_ref.shape[1], x_ref.shape[2]
    hidden_width = win_ref.shape[3]
    at = lax.broadcasted_iota(jnp.int32, (slots, tokens), 0)
    mask = at == slot_ref[0, 0]
    pick = jnp.where(mask, 1.0, 0.0).astype(BF16)
    gate = jnp.sum(jnp.where(mask, prob_ref[0, 0], 0.0), axis=1, keepdims=True)
    rows = dot(pick, x_ref[0], 1, 0).astype(BF16)
    grows = dot(pick, grad_ref[0], 1, 0).astype(BF16)
    rows_ref[0, 0] = rows
    grows_ref[0, 0] = grows
    dgate = jnp.zeros((slots, 1), F32)
    drows = jnp.zeros((slots, model), F32)
    yrows = jnp.zeros((slots, model), F32)
    tile = 512 if hidden_width % 512 == 0 else hidden_width
    curve = 0.7978845608028654
    for start in range(0, hidden_width, tile):
        cols = slice(start, start + tile)
        win = win_ref[:, 0, :, cols].reshape(model, tile)
        wout = wout_ref[:, 0, :, cols].reshape(model, tile)
        hidden = dot(rows, win, 1, 0)
        pulled = dot(grows, wout, 1, 0)
        square = hidden * hidden
        bend = jnp.tanh(hidden * (curve + curve * 0.044715 * square))
        half = 0.5 + 0.5 * bend
        active = hidden * half
        slope = half + 0.5 * hidden * (1.0 - bend * bend) * (
            curve + 3.0 * curve * 0.044715 * square
        )
        dgate = dgate + jnp.sum(active * pulled, axis=1, keepdims=True)
        gact = (gate * active).astype(BF16)
        dhid = (gate * pulled * slope).astype(BF16)
        gact_ref[0, 0, :, cols] = gact
        dhid_ref[0, 0, :, cols] = dhid
        drows = drows + dot(dhid, win, 1, 1)
        yrows = yrows + dot(gact, wout, 1, 1)
    dgate_ref[0, 0] = dgate
    drows_ref[0, 0] = drows.astype(BF16)
    yrows_ref[0, 0] = yrows.astype(BF16)


def run_experts(slot_of, probs, tokens_all, grads_all, w_in, w_out, slots):
    blocks, local, _, tokens = slot_of.shape
    model = tokens_all.shape[2]
    depth, _, part_rows, width = w_in.shape
    pair = lambda e, b: (b, e, 0, 0)
    block = lambda e, b: (b, 0, 0)
    weight = pl.BlockSpec((depth, 1, part_rows, width), lambda e, b: (0, e, 0, 0))
    shape = lambda last, kind: jax.ShapeDtypeStruct((blocks, local, slots, last), kind)
    spec = lambda last: pl.BlockSpec((1, 1, slots, last), pair)
    return pl.pallas_call(
        expert_kernel,
        grid=(local, blocks),
        in_specs=[
            pl.BlockSpec((1, 1, 1, tokens), pair),
            pl.BlockSpec((1, 1, 1, tokens), pair),
            pl.BlockSpec((1, tokens, model), block),
            pl.BlockSpec((1, tokens, model), block),
            weight,
            weight,
        ],
        out_specs=[
            spec(model), spec(model), spec(width), spec(width), spec(1), spec(model), spec(model)
        ],
        out_shape=[
            shape(model, BF16), shape(model, BF16), shape(width, BF16), shape(width, BF16),
            shape(1, F32), shape(model, BF16), shape(model, BF16),
        ],
        compiler_params=params(2),
        cost_estimate=pl.CostEstimate(
            flops=8 * blocks * local * slots * model * width
            + 4 * blocks * local * slots * model * tokens,
            bytes_accessed=16 * blocks * local * slots * model,
            transcendentals=blocks * local * slots * width,
        ),
        name="experts",
    )(slot_of, probs, tokens_all, grads_all, w_in, w_out)


def weight_grad_kernel(rows_ref, cols_ref, out_ref):
    blocks, _, slots, model = rows_ref.shape
    depth, _, part_rows, tile = out_ref.shape
    left = rows_ref[...].reshape(blocks * slots, model)
    right = cols_ref[...].reshape(blocks * slots, tile)
    out_ref[...] = dot(left, right, 0, 0).astype(BF16).reshape(depth, 1, part_rows, tile)


def weight_grad(rows, cols, depth):
    blocks, local, slots, model = rows.shape
    width = cols.shape[3]
    tile = width // 2 if width % 256 == 0 else width
    return pl.pallas_call(
        weight_grad_kernel,
        grid=(local, width // tile),
        in_specs=[
            pl.BlockSpec((blocks, 1, slots, model), lambda e, f: (0, e, 0, 0)),
            pl.BlockSpec((blocks, 1, slots, tile), lambda e, f: (0, e, 0, f)),
        ],
        out_specs=pl.BlockSpec((depth, 1, model // depth, tile), lambda e, f: (0, e, 0, f)),
        out_shape=jax.ShapeDtypeStruct((depth, local, model // depth, width), BF16),
        compiler_params=params(2),
        cost_estimate=pl.CostEstimate(
            flops=2 * blocks * local * slots * model * width,
            bytes_accessed=2 * local * (blocks * slots * (model + width) + model * width),
            transcendentals=0,
        ),
        name="weight_grad",
    )(rows, cols)


def combine_kernel(slot_ref, rows_ref, out_ref):
    _, local, slots, model = rows_ref.shape
    tokens = out_ref.shape[1]
    at = lax.broadcasted_iota(jnp.int32, (tokens, slots), 1)
    total = jnp.zeros((tokens, model), F32)
    for e in range(local):
        pick = jnp.where(at == slot_ref[0, :, e : e + 1], 1.0, 0.0).astype(BF16)
        total = total + dot(pick, rows_ref[0, e], 1, 0)
    out_ref[0] = total.astype(BF16)


def combine_add_kernel(slot_ref, rows_ref, dlog_ref, router_ref, out_ref):
    _, local, slots, model = rows_ref.shape
    tokens = out_ref.shape[1]
    at = lax.broadcasted_iota(jnp.int32, (tokens, slots), 1)
    total = dot(dlog_ref[0], router_ref[...], 0, 1)
    for e in range(local):
        pick = jnp.where(at == slot_ref[0, :, e : e + 1], 1.0, 0.0).astype(BF16)
        total = total + dot(pick, rows_ref[0, e], 1, 0)
    out_ref[0] = total.astype(BF16)


def combine(slot_cols, rows, extra=None):
    blocks, tokens, local = slot_cols.shape
    slots, model = rows.shape[2:]
    in_specs = [
        pl.BlockSpec((1, tokens, local), lambda b: (b, 0, 0)),
        pl.BlockSpec((1, local, slots, model), lambda b: (b, 0, 0, 0)),
    ]
    args = (slot_cols, rows)
    if extra is not None:
        dlog, router = extra
        in_specs += [
            pl.BlockSpec((1,) + dlog.shape[1:], lambda b: (b, 0, 0)),
            pl.BlockSpec(router.shape, lambda b: (0, 0)),
        ]
        args += extra
    return pl.pallas_call(
        combine_kernel if extra is None else combine_add_kernel,
        grid=(blocks,),
        in_specs=in_specs,
        out_specs=pl.BlockSpec((1, tokens, model), lambda b: (b, 0, 0)),
        out_shape=jax.ShapeDtypeStruct((blocks, tokens, model), BF16),
        compiler_params=params(1),
        cost_estimate=pl.CostEstimate(
            flops=2 * blocks * local * slots * model * tokens,
            bytes_accessed=2 * blocks * model * (local * slots + tokens),
            transcendentals=0,
        ),
        name="combine",
    )(*args)


def per_device(
    block_in, cotangent, route_ids, gain_attn, w_qkv, w_out_attn, gain_moe, router, w_in, w_out
):
    n_dp, n_heads, n_exp = (lax.axis_size(name) for name in ("dp", "heads", "expert"))
    n_z = n_dp // CORES
    dp, head, exp = (lax.axis_index(name) for name in ("dp", "heads", "expert"))
    z, core = dp // CORES, dp % CORES
    images, seq, half_width = block_in.shape
    tokens = images * seq
    model = half_width * n_heads
    width = w_qkv.shape[2]
    expert_count = router.shape[1]
    group = w_in.shape[1]
    local = group // CORES
    hidden_width = w_in.shape[2]
    capacity = 20 * tokens // (7 * expert_count)
    slots = -(-capacity // 16) * 16

    def shift(value, axis, step):
        size = lax.axis_size(axis)
        return lax.ppermute(value, axis, [(i, (i + step) % size) for i in range(size)])

    def shift_z(value, step):
        pairs = [
            (a * CORES + c, ((a + step) % n_z) * CORES + c) for a in range(n_z) for c in range(CORES)
        ]
        return lax.ppermute(value, "dp", pairs)

    def swap_core(value):
        return lax.ppermute(value, "dp", [(i, i ^ 1) for i in range(n_dp)])

    def place(pieces, index, count):
        if count == 2:
            first = index == 0
            return jnp.stack(
                [jnp.where(first, pieces[0], pieces[1]), jnp.where(first, pieces[1], pieces[0])]
            )
        out = jnp.zeros((count,) + pieces[0].shape, pieces[0].dtype)
        for k, piece in enumerate(pieces):
            out = lax.dynamic_update_index_in_dim(out, piece, (index - k) % count, 0)
        return out

    def spread(value, axis):
        return [value] + [shift(value, axis, k) for k in range(1, lax.axis_size(axis))]

    def take(value, index, dim=0):
        return lax.dynamic_index_in_dim(value, index, dim, keepdims=False)

    rest = 128
    tail = jnp.concatenate(
        [router, gain_attn[:, None], gain_moe[:, None],
         jnp.zeros((router.shape[0], rest - expert_count - 2), BF16)], axis=1
    )
    own_pack = jnp.concatenate(
        [w_qkv.reshape(w_qkv.shape[0], 3 * width), w_out_attn, tail], axis=1
    )
    pack = place(spread(own_pack, "expert"), exp, n_exp)
    pack = place([pack] + [shift_z(pack, k) for k in range(1, n_z)], z, n_z)
    other_pack = swap_core(pack)
    low = core == 0
    pack = jnp.stack(
        [jnp.where(low, pack, other_pack), jnp.where(low, other_pack, pack)], axis=1
    ).reshape(model, own_pack.shape[1])
    side = pack[:, 4 * width :]
    router_all = side[:, :expert_count]
    gain_one = side[:, expert_count].astype(F32)[None, :]
    gain_two = side[:, expert_count + 1].astype(F32)[None, :]

    def full_rows(value):
        parts = place(spread(value, "heads"), head, n_heads)
        return jnp.concatenate([parts[i] for i in range(n_heads)], axis=-1)

    inputs = full_rows(block_in)

    def expert_weight(weight):
        by_core = weight.reshape(weight.shape[0], CORES, local, hidden_width).transpose(1, 2, 0, 3)
        other = swap_core(take(by_core, 1 - core))
        mine = take(by_core, core)
        piece = jnp.concatenate(
            [jnp.where(low, mine, other), jnp.where(low, other, mine)], axis=1
        )
        pieces = [piece]
        for _ in range(1, n_z):
            pieces.append(shift_z(pieces[-1], 1))
        return place(pieces, z, n_z)

    out_all = expert_weight(w_out)
    in_all = expert_weight(w_in)

    def blocks_of(value):
        along = jnp.stack(spread(value, "expert"))
        return jnp.concatenate([along, swap_core(along)])

    grad_full = full_rows(cotangent).reshape(tokens, model)
    grads_all = blocks_of(grad_full)
    ids = route_ids.reshape(tokens, 2).T
    ids_all = blocks_of(ids)
    blocks = n_exp * CORES
    first_expert = exp * group + core * local
    named = first_expert + jnp.arange(local, dtype=jnp.int32)
    chosen = jnp.any(ids_all[:, None, :, :] == named[None, :, None, None], axis=2)
    before = (
        jnp.arange(tokens)[:, None] < jnp.arange(tokens)[None, :]
    ).astype(BF16)
    rank = jnp.dot(
        chosen.astype(BF16).reshape(blocks * local, tokens), before, preferred_element_type=F32
    ).astype(jnp.int32).reshape(blocks, local, tokens)
    slot_of = jnp.where(chosen, rank, -1)
    slot_cols = slot_of.transpose(0, 2, 1)

    part, qkv, ctx = attend(inputs, gain_one, pack, width)
    part_other = shift(part, "heads", 1)
    for k in range(2, n_heads):
        part_other = part_other + shift(part, "heads", k)
    middle = (inputs.astype(F32) + (part.astype(F32) + part_other.astype(F32))).reshape(
        tokens, model
    )
    unit_two, scale_two = norm_parts(middle)
    normed_two = (unit_two * gain_two).astype(BF16)
    tokens_all = blocks_of(normed_two)

    logits = jnp.einsum("de,btd->bet", router_all, tokens_all, preferred_element_type=F32)
    probs = jax.nn.softmax(logits, axis=1)
    own_probs = lax.dynamic_slice_in_dim(probs, first_expert, local, 1)

    rows, grows, gact, dhid, dgate, drows, yrows = run_experts(
        slot_of[:, :, None, :], own_probs[:, :, None, :], tokens_all, grads_all, in_all, out_all, slots
    )

    def ring_sum(total):
        moving = take(total, (z - 1) % n_z)
        for step in range(1, n_z):
            arrived = shift_z(moving, 1)
            mine = take(total, (z - 1 - step) % n_z)
            moving = arrived.astype(F32) + mine.astype(F32)
            if step < n_z - 1:
                moving = moving.astype(BF16)
        halves = moving.reshape(local, CORES, w_in.shape[0], hidden_width)
        other = swap_core(take(halves, 1 - core, 1).astype(BF16)).astype(F32)
        mine = take(halves, core, 1)
        joined = jnp.concatenate(
            [jnp.where(low, mine, other), jnp.where(low, other, mine)], axis=0
        )
        return joined.transpose(1, 0, 2)

    grad_w_in = ring_sum(weight_grad(rows, dhid, n_z))
    grad_w_out = ring_sum(weight_grad(grows, gact, n_z))

    at = jnp.arange(slots, dtype=jnp.int32)
    dchosen = jnp.sum(
        jnp.where(slot_of[:, :, None, :] == at[None, None, :, None], dgate, 0.0), axis=2
    )
    dprobs = lax.dynamic_update_slice_in_dim(jnp.zeros_like(probs), dchosen, first_expert, 1)
    dlogits = (probs * (dprobs - jnp.sum(dprobs * probs, axis=1, keepdims=True))).astype(BF16)
    grad_router = jnp.einsum("btd,bet->de", tokens_all, dlogits, preferred_element_type=F32)

    def home(partial):
        keep, send = partial[:n_exp], partial[n_exp:]
        total = keep.astype(F32) + swap_core(send).astype(F32)
        own = total[0]
        for k in range(1, n_exp):
            own = own + shift(total[k].astype(BF16), "expert", -k).astype(F32)
        return own

    dsum = home(combine(slot_cols, drows, (dlogits, router_all))).astype(BF16)
    dsum_other = shift(dsum, "heads", 1)
    for k in range(2, n_heads):
        dsum_other = dsum_other + shift(dsum, "heads", k)
    dnormed_two = dsum.astype(F32) + dsum_other.astype(F32)
    scaled = dnormed_two * gain_two
    grad_gain_two = jnp.sum(dnormed_two * unit_two, axis=0)
    dmiddle = grad_full.astype(F32) + scale_two * (
        scaled
        - jnp.mean(scaled, axis=-1, keepdims=True)
        - unit_two * jnp.mean(scaled * unit_two, axis=-1, keepdims=True)
    )
    datt = dmiddle.astype(BF16).reshape(images, seq, model)

    yrows, datt = lax.optimization_barrier((yrows, datt))
    y_own = home(combine(slot_cols, yrows)).astype(BF16)
    y_parts = y_own.reshape(tokens, n_heads, half_width).transpose(1, 0, 2)
    y_total = take(y_parts, head).astype(F32)
    for k in range(1, n_heads):
        y_total = y_total + shift(take(y_parts, (head + k) % n_heads), "heads", k).astype(F32)
    middle_own = lax.dynamic_slice_in_dim(middle, head * half_width, half_width, 1)
    block_out = (middle_own + y_total).astype(BF16).reshape(images, seq, half_width)

    dnorm, stats, dgain_one, dw_qkv, dw_o = attend_back(
        inputs, gain_one, datt, qkv, ctx, pack, width
    )
    dn_parts = dnorm.reshape(tokens, n_heads, half_width).transpose(1, 0, 2)
    dn_own = take(dn_parts, head).astype(F32)
    sums = stats.reshape(tokens, 128)[:, :2].T
    sums_total = sums
    for k in range(1, n_heads):
        dn_own = dn_own + shift(take(dn_parts, (head + k) % n_heads), "heads", k).astype(F32)
        sums_total = sums_total + shift(sums, "heads", k)
    unit_one, scale_one = norm_parts(inputs.astype(F32).reshape(tokens, model))
    unit_own = lax.dynamic_slice_in_dim(unit_one, head * half_width, half_width, 1)
    gain_own = lax.dynamic_slice_in_dim(gain_one, head * half_width, half_width, 1)
    dmiddle_own = lax.dynamic_slice_in_dim(dmiddle, head * half_width, half_width, 1)
    grad_in = dmiddle_own + scale_one * (
        dn_own * gain_own
        - sums_total[0][:, None] / model
        - unit_own * (sums_total[1][:, None] / model)
    )
    grad_block_in = grad_in.astype(BF16).reshape(images, seq, half_width)

    dside = jnp.concatenate(
        [grad_router, dgain_one.T, grad_gain_two[:, None],
         jnp.zeros((model, rest - expert_count - 2), F32)], axis=1
    )
    dpack = jnp.concatenate(
        [dw_qkv.astype(BF16), dw_o.astype(BF16), dside.astype(BF16)], axis=1
    ).reshape(n_z, CORES, n_exp, own_pack.shape[0], own_pack.shape[1])
    dsent = swap_core(take(dpack, 1 - core, 1))
    dpack = (take(dpack, core, 1).astype(F32) + dsent.astype(F32)).astype(BF16)
    dtotal = take(dpack, exp, 1).astype(F32)
    for k in range(1, n_exp):
        dtotal = dtotal + shift(take(dpack, (exp + k) % n_exp, 1), "expert", k).astype(F32)
    dpack = dtotal.astype(BF16)
    dtotal = take(dpack, z).astype(F32)
    for k in range(1, n_z):
        dtotal = dtotal + shift_z(take(dpack, (z + k) % n_z), k).astype(F32)
    dside = dtotal[:, 4 * width :]
    over_heads = dside[:, : expert_count + 1].T
    summed = over_heads
    for k in range(1, n_heads):
        summed = summed + shift(over_heads, "heads", k)
    return (
        block_out,
        grad_block_in,
        summed[expert_count],
        dtotal[:, : 3 * width].reshape(-1, 3, width),
        dtotal[:, 3 * width : 4 * width],
        dside[:, expert_count + 1],
        summed[:expert_count].T,
        grad_w_in,
        grad_w_out,
    )


def solution(mesh):
    return jax.shard_map(
        per_device,
        mesh=mesh,
        in_specs=(
            P(("dp", "expert"), None, "heads"),
            P(("dp", "expert"), None, "heads"),
            P(("dp", "expert"), None, None),
            P(("dp", "expert")),
            P(("dp", "expert"), None, "heads"),
            P(("dp", "expert"), "heads"),
            P(("dp", "expert")),
            P(("dp", "expert"), None),
            P("dp", "expert", "heads"),
            P("dp", "expert", "heads"),
        ),
        out_specs=(
            P(("dp", "expert"), None, "heads"),
            P(("dp", "expert"), None, "heads"),
            P(("dp", "expert")),
            P(("dp", "expert"), None, "heads"),
            P(("dp", "expert"), "heads"),
            P(("dp", "expert")),
            P(("dp", "expert"), None),
            P("dp", "expert", "heads"),
            P("dp", "expert", "heads"),
        ),
        check_vma=False,
    )
```

time: 1260 us -> 630 us (0.50)
  waiting for transfers between devices: 609 us -> 275 us
  blocking collectives: 155 us -> 0 us
  local copies, waits for them, and re-layouts: 265 us -> 115 us
  matrix products: 130 us -> 4.89 us
  Pallas kernels: 0 us -> 112 us
  other arithmetic: 49.2 us -> 72.9 us
  starting transfers between devices: 21.2 us -> 39.2 us
  between operations: 17.5 us -> 2.47 us
    unnamed x18 -> x0, waiting for transfers between devices: 379 us -> none
    ppermute x0 -> x44, waiting for transfers between devices: none -> 275 us  [the longest x18 220 us: shift_z(): return lax.ppermute(value, 'dp', pairs)]
    dot_general x20 -> x2, matrix products: 127 us -> 1.03 us  [the longest x1 0.77 us: per_device(): jnp.einsum('btd,bet->de', tokens_all, dlogits, preferred_element_type=F32)]
    pallas_call x0 -> x7, Pallas kernels: none -> 112 us  [the longest x1 40.7 us: run_experts(): pl.pallas_call(expert_kernel, grid=(local, blocks), in_specs=[pl.BlockSpe...]
    reduce_scatter x2 -> x0, waiting for transfers between devices: 93.2 us -> none  [the longest x1 71.3 us: per_device(): lax.psum_scatter(grad_qkv_weight, ('dp', 'expert'), scatter_dimension=0,...]
    unnamed x2 -> x0, blocking collectives: 68.7 us -> none
    all_gather x2 -> x0, blocking collectives: 64.5 us -> none  [the longest x1 33.6 us: per_device(): lax.all_gather(w_out_attn, ('dp', 'expert'), axis=0, tiled=True)]
    gather x7 -> x0, local copies, waits for them, and re-layouts: 57.2 us -> none  [the longest x2 15.8 us: per_device(): normed_two[source_rows]]
  transfers between devices with their start and end apart: 18 -> 44, of which waited for: 9 -> 21; matrix products, arithmetic and copies ran while one was open for 28% -> 24% of each run, Pallas kernels for 0% -> 5%
where the time goes in v1:
time: 630 us; the launch traced here: 621 us
  waiting for transfers between devices  275 us (44%)
  local copies, waits for them, and re-layouts  115 us (18%)
  Pallas kernels  112 us (18%)
  other arithmetic  72.9 us (12%)
  starting transfers between devices  39.2 us (6%)
    ppermute x18, waiting for transfers between devices, shift_z(): return lax.ppermute(value, 'dp', pairs)  220 us
    ppermute x15, waiting for transfers between devices, shift(): lax.ppermute(value, axis, [(i, (i + step) % size) for i in range(size)])  53.5 us
    pallas_call x1, Pallas kernels, run_experts(): pl.pallas_call(expert_kernel, grid=(local, blocks), in_specs=[pl.BlockSpe...  40.7 us
    pallas_call x2, Pallas kernels, weight_grad(): pl.pallas_call(weight_grad_kernel, grid=(local, width // tile), in_specs=...  21.7 us
    pallas_call x1, Pallas kernels, attend_back(): pl.pallas_call(attend_back_kernel, grid=(images,), in_specs=[pl.BlockSpec...  20.1 us
    ppermute x15, starting transfers between devices, shift(): lax.ppermute(value, axis, [(i, (i + step) % size) for i in range(size)])  19.8 us
    pallas_call x2, Pallas kernels, combine(): pl.pallas_call(combine_kernel if extra is None else combine_add_kernel, g...  19.1 us
    ppermute x18, starting transfers between devices, shift_z(): return lax.ppermute(value, 'dp', pairs)  17.9 us
  transfers between devices with their start and end apart: 44, of which 21 were waited for; matrix products, arithmetic and copies ran while one was open for 24% of the time, Pallas kernels for 5%

profile of v1, /device:TPU:0, one launch (start us, length us, event | category | flops | bytes accessed | tf_op | source)
XLA Modules:
  0.0 621.0 jit_solution(10725651750729179163)
XLA Ops:
  19.2 7.4 %collective-permute-done.2 = bf16[2,48,1664]{2,1,0:T(8,128)(2,1)} collective-permute-done((bf16[2,48,1664]{2,1,0:T(8,128)(2,1)}, bf16[2,48,1664]{2,1,0:T(8,128)(2,1)}, u32[]{:S(2)}, u32[]{:S(2)}) %collective-permute-start.2) | collective-permute-done | bytes 319520 | tf_op jit(solution)/shard_map/ppermute | solution.py:386
  28.4 13.6 %collective-permute-done.3 = bf16[2,48,1664]{2,1,0:T(8,128)(2,1)S(1)} collective-permute-done((bf16[2,48,1664]{2,1,0:T(8,128)(2,1)}, bf16[2,48,1664]{2,1,0:T(8,128)(2,1)S(1)}, u32[]{:S(2)}, u32[]{:S(2)}) %collective-permute-start.3) | collective-permute-done | bytes 319520 | tf_op jit(solution)/shard_map/ppermute | solution.py:386
  44.5 7.2 %collective-permute-done.4 = bf16[2,48,1664]{2,1,0:T(8,128)(2,1)S(1)} collective-permute-done((bf16[2,48,1664]{2,1,0:T(8,128)(2,1)}, bf16[2,48,1664]{2,1,0:T(8,128)(2,1)S(1)}, u32[]{:S(2)}, u32[]{:S(2)}) %collective-permute-start.4) | collective-permute-done | bytes 319520 | tf_op jit(solution)/shard_map/ppermute | solution.py:386
  62.7 10.7 %attend.1 = (bf16[4,197,768]{2,1,0:T(8,128)(2,1)}, bf16[4,197,1152]{2,1,0:T(8,128)(2,1)}, bf16[4,197,384]{2,1,0:T(8,128)(2,1)}) custom-call(bf16[4,197,768]{2,1,0:T(8,128)(2,1)} %pad_maximum_fusion.5.x_ref, f32[1,768]{1,0:T(1,128)} %reshape.334.gain_ref, bf16[768,1664]{1,0:T(8,128)(2,1)} %bitcast.215, bf16[768,1664]{1,0:T(8,128)(2,1)} %bitcast.216), custom_call_target="tpu_custom_call" | custom-call | flops 2323906560 | bytes 4841472 | tf_op jit(solution)/shard_map/attend/pallas_call | solution.py:66
  96.8 14.1 %collective-permute-done.15 = bf16[2,192,1536]{2,1,0:T(8,128)(2,1)} collective-permute-done((bf16[2,192,1536]{2,1,0:T(8,128)(2,1)}, bf16[2,192,1536]{2,1,0:T(8,128)(2,1)}, u32[]{:S(2)}, u32[]{:S(2)}) %collective-permute-start.15) | collective-permute-done | bytes 1179680 | tf_op jit(solution)/shard_map/ppermute | solution.py:386
  129.6 6.5 %collective-permute-done.20 = bf16[2,192,1536]{2,1,0:T(8,128)(2,1)} collective-permute-done((bf16[2,192,1536]{2,1,0:T(8,128)(2,1)}, bf16[2,192,1536]{2,1,0:T(8,128)(2,1)}, u32[]{:S(2)}, u32[]{:S(2)}) %collective-permute-start.20) | collective-permute-done | bytes 1179680 | tf_op jit(solution)/shard_map/ppermute | solution.py:386
  136.2 25.3 %collective-permute-done.16 = bf16[2,192,1536]{2,1,0:T(8,128)(2,1)} collective-permute-done((bf16[2,192,1536]{2,1,0:T(8,128)(2,1)}, bf16[2,192,1536]{2,1,0:T(8,128)(2,1)}, u32[]{:S(2)}, u32[]{:S(2)}) %collective-permute-start.16) | collective-permute-done | bytes 1179680 | tf_op jit(solution)/shard_map/ppermute | solution.py:386
  175.1 11.6 %collective-permute-done.21 = bf16[2,192,1536]{2,1,0:T(8,128)(2,1)} collective-permute-done((bf16[2,192,1536]{2,1,0:T(8,128)(2,1)}, bf16[2,192,1536]{2,1,0:T(8,128)(2,1)}, u32[]{:S(2)}, u32[]{:S(2)}) %collective-permute-start.21) | collective-permute-done | bytes 1179680 | tf_op jit(solution)/shard_map/ppermute | solution.py:386
  189.1 22.6 %collective-permute-done.17 = bf16[2,192,1536]{2,1,0:T(8,128)(2,1)} collective-permute-done((bf16[2,192,1536]{2,1,0:T(8,128)(2,1)}, bf16[2,192,1536]{2,1,0:T(8,128)(2,1)}, u32[]{:S(2)}, u32[]{:S(2)}) %collective-permute-start.17) | collective-permute-done | bytes 1179680 | tf_op jit(solution)/shard_map/ppermute | solution.py:386
  228.4 40.7 %experts.1 = (bf16[4,2,288,768]{3,2,1,0:T(8,128)(2,1)}, bf16[4,2,288,768]{3,2,1,0:T(8,128)(2,1)}, bf16[4,2,288,1536]{3,2,1,0:T(8,128)(2,1)}, bf16[4,2,288,1536]{...) custom-call(s32[4,2,1,788]{3,2,1,0:T(1,128)} %copy_select_fusion.slo, ...), custom_call_target="tpu_custom_call" | custom-call | flops 27320647680 | bytes 28311552 | tf_op jit(solution)/shard_map/experts/pallas_call | solution.py:247
  269.1 10.8 %weight_grad.3 = bf16[4,2,192,1536]{3,2,1,0:T(8,128)(2,1)} custom-call(bf16[4,2,288,768]{3,2,1,0:T(8,128)(2,1)} %get-tuple-element.41.rows_ref, bf16[4,2,288,1536]{3,2,1,0:T(8,128)(2,1)} %get-tuple-element.42.cols_ref), custom_call_target="tpu_custom_call" | custom-call | flops 5435817984 | bytes 15335424 | tf_op jit(solution)/shard_map/weight_grad/pallas_call | solution.py:288
  282.8 10.8 %weight_grad.2 = bf16[4,2,192,1536]{3,2,1,0:T(8,128)(2,1)} custom-call(bf16[4,2,288,768]{3,2,1,0:T(8,128)(2,1)} %get-tuple-element.39.rows_ref, bf16[4,2,288,1536]{3,2,1,0:T(8,128)(2,1)} %get-tuple-element.40.cols_ref), custom_call_target="tpu_custom_call" | custom-call | flops 5435817984 | bytes 15335424 | tf_op jit(solution)/shard_map/weight_grad/pallas_call | solution.py:288
  302.0 10.4 %combine.2 = bf16[4,788,768]{2,1,0:T(8,128)(2,1)} custom-call(s32[4,788,2]{2,1,0:T(8,128)} %bitcast.212, bf16[4,2,288,768]{3,2,1,0:T(8,128)(2,1)} %get-tuple-element.28.rows_ref, bf16[4,8,788]{2,1,0:T(8,128)(2,1)} %multiply_convert_fusion.2.dlog_ref, bf16[768,8]{1,0:T(8,128)(2,1)} %slice.91.router_ref), custom_call_target="tpu_custom_call" | custom-call | flops 2788687872 | bytes 8380416 | tf_op jit(solution)/shard_map/combine/pallas_call | solution.py:344
  319.1 19.9 %collective-permute-done.36 = bf16[2,192,1536]{2,1,0:T(8,128)(2,1)} collective-permute-done((bf16[2,192,1536]{2,1,0:T(8,128)(2,1)}, bf16[2,192,1536]{2,1,0:T(8,128)(2,1)}, u32[]{:S(2)}, u32[]{:S(2)}) %collective-permute-start.36) | collective-permute-done | bytes 1179680 | tf_op jit(solution)/shard_map/ppermute | solution.py:386
  344.7 19.5 %collective-permute-done.41 = bf16[2,192,1536]{2,1,0:T(8,128)(2,1)S(1)} collective-permute-done((bf16[2,192,1536]{2,1,0:T(8,128)(2,1)S(1)}, bf16[2,192,1536]{2,1,0:T(8,128)(2,1)S(1)}, u32[]{:S(2)}, u32[]{:S(2)}) %collective-permute-start.41) | collective-permute-done | bytes 1179680 | tf_op jit(solution)/shard_map/ppermute | solution.py:386
  364.6 24.9 %collective-permute-done.37 = bf16[2,192,1536]{2,1,0:T(8,128)(2,1)S(1)} collective-permute-done((bf16[2,192,1536]{2,1,0:T(8,128)(2,1)S(1)}, bf16[2,192,1536]{2,1,0:T(8,128)(2,1)S(1)}, u32[]{:S(2)}, u32[]{:S(2)}) %collective-permute-start.37) | collective-permute-done | bytes 1179680 | tf_op jit(solution)/shard_map/ppermute | solution.py:386
  392.4 22.3 %collective-permute-done.42 = bf16[2,192,1536]{2,1,0:T(8,128)(2,1)S(1)} collective-permute-done((bf16[2,192,1536]{2,1,0:T(8,128)(2,1)S(1)}, bf16[2,192,1536]{2,1,0:T(8,128)(2,1)S(1)}, u32[]{:S(2)}, u32[]{:S(2)}) %collective-permute-start.42) | collective-permute-done | bytes 1179680 | tf_op jit(solution)/shard_map/ppermute | solution.py:386
  416.0 22.9 %collective-permute-done.38 = bf16[2,192,1536]{2,1,0:T(8,128)(2,1)S(1)} collective-permute-done((bf16[2,192,1536]{2,1,0:T(8,128)(2,1)S(1)}, bf16[2,192,1536]{2,1,0:T(8,128)(2,1)S(1)}, u32[]{:S(2)}, u32[]{:S(2)}) %collective-permute-start.38) | collective-permute-done | bytes 1179680 | tf_op jit(solution)/shard_map/ppermute | solution.py:386
  450.0 21.0 %collective-permute-done.24 = bf16[788,768]{1,0:T(8,128)(2,1)} collective-permute-done((bf16[788,768]{1,0:T(8,128)(2,1)}, bf16[788,768]{1,0:T(8,128)(2,1)}, u32[]{:S(2)}, u32[]{:S(2)}) %collective-permute-start.24) | collective-permute-done | bytes 1210400 | tf_op jit(solution)/shard_map/ppermute | solution.py:380
  480.2 20.1 %attend_back.1 = (bf16[4,197,768]{2,1,0:T(8,128)(2,1)}, f32[4,197,128]{2,1,0:T(8,128)}, f32[1,768]{1,0:T(1,128)}, f32[768,1152]{1,0:T(8,128)}, f32[768,384]{1,0:T(8,128)}) custom-call(bf16[4,197,768]{2,1,0:T(8,128)(2,1)} %pad_maximum_fusion.5.x_ref, f32[1,768]{1,0:T(1,128)} %reshape.334.gain_ref, bf16[4,197,768]{2,1,0:T(8,128)(2,1)} %reshape.323.datt_ref, ...), custom_call_target="tpu_custom_call" | custom-call | flops 6506938368 | bytes 9682944 | tf_op jit(solution)/shard_map/attend_back/pallas_call | solution.py:156
  504.9 8.7 %combine.3 = bf16[4,788,768]{2,1,0:T(8,128)(2,1)} custom-call(s32[4,788,2]{2,1,0:T(8,128)} %bitcast.213, bf16[4,2,288,768]{3,2,1,0:T(8,128)(2,1)} %get-tuple-element.30.rows_ref), custom_call_target="tpu_custom_call" | custom-call | flops 2788687872 | bytes 8380416 | tf_op jit(solution)/shard_map/combine/pallas_call | solution.py:344
  554.8 11.2 %collective-permute-done.31 = bf16[4,48,1664]{2,1,0:T(8,128)(2,1)S(1)} collective-permute-done((bf16[4,48,1664]{2,1,0:T(8,128)(2,1)S(1)}, bf16[4,48,1664]{2,1,0:T(8,128)(2,1)S(1)}, u32[]{:S(2)}, u32[]{:S(2)}) %collective-permute-start.31) | collective-permute-done | bytes 639008 | tf_op jit(solution)/shard_map/ppermute | solution.py:380
  580.5 9.8 %collective-permute-done.26 = bf16[788,768]{1,0:T(8,128)(2,1)} collective-permute-done((bf16[788,768]{1,0:T(8,128)(2,1)}, bf16[788,768]{1,0:T(8,128)(2,1)}, u32[]{:S(2)}, u32[]{:S(2)}) %collective-permute-start.26) | collective-permute-done | bytes 1210400 | tf_op jit(solution)/shard_map/ppermute | solution.py:380
  608.5 9.2 %collective-permute-done.27 = bf16[788,384]{1,0:T(8,128)(2,1)} collective-permute-done((bf16[788,384]{1,0:T(8,128)(2,1)}, bf16[788,384]{1,0:T(8,128)(2,1)}, u32[]{:S(2)}, u32[]{:S(2)}) %collective-permute-start.27) | collective-permute-done | bytes 605216 | tf_op jit(solution)/shard_map/ppermute | solution.py:380
  (347 shorter events, 237.0 us)
Async XLA Ops:
  3.2 48.7 %collective-permute-start.18 = (bf16[2,96,1536]{2,1,0:T(8,128)(2,1)}, bf16[2,96,1536]{2,1,0:T(8,128)(2,1)}, u32[]{:S(2)}, u32[]{:S(2)}) collective-permute-start(bf16[2,96,1536]{2,1,0:T(8,128)(2,1)} %dynamic-slice_bitcast_fusion.4), channel_id=1, source_target_pairs={{0,4},{4,0},{8,12},{12,8},{16,20},{20,16},{24,28},{28,24},{1,5},{5... | collective-permute-start | bytes 1769480 | tf_op jit(solution)/shard_map/ppermute | solution.py:389
  7.5 46.8 %collective-permute-start.14 = (bf16[2,96,1536]{2,1,0:T(8,128)(2,1)}, bf16[2,96,1536]{2,1,0:T(8,128)(2,1)}, u32[]{:S(2)}, u32[]{:S(2)}) collective-permute-start(bf16[2,96,1536]{2,1,0:T(8,128)(2,1)} %dynamic-slice_bitcast_fusion.5), channel_id=1, source_target_pairs={{0,4},{4,0},{8,12},{12,8},{16,20},{20,16},{24,28},{28,24},{1,5},{5... | collective-permute-start | bytes 1769480 | tf_op jit(solution)/shard_map/ppermute | solution.py:389
  8.5 46.9 %collective-permute-start = (bf16[4,197,384]{2,0,1:T(4,128)(2,1)}, bf16[4,197,384]{2,0,1:T(4,128)(2,1)}, u32[]{:S(2)}, u32[]{:S(2)}) collective-permute-start(bf16[4,197,384]{2,0,1:T(4,128)(2,1)} %param.10), channel_id=1, source_target_pairs={{0,2},{2,0},{1,3},{3,1},{4,6},{6,4},{5,7},{7,5},{8,10},{10,8},{9,1... | collective-permute-start | bytes 1815560 | tf_op jit(solution)/shard_map/ppermute | solution.py:380
  11.5 43.9 %collective-permute-start.11 = (bf16[4,197,384]{2,0,1:T(4,128)(2,1)}, bf16[4,197,384]{2,0,1:T(4,128)(2,1)}, u32[]{:S(2)}, u32[]{:S(2)}) collective-permute-start(bf16[4,197,384]{2,0,1:T(4,128)(2,1)} %param.11), channel_id=1, source_target_pairs={{0,2},{2,0},{1,3},{3,1},{4,6},{6,4},{5,7},{7,5},{8,10},{10,8},{9,1... | collective-permute-start | bytes 1815560 | tf_op jit(solution)/shard_map/ppermute | solution.py:380
  54.3 39.0 %collective-permute-start.19 = (bf16[2,192,1536]{2,1,0:T(8,128)(2,1)}, bf16[2,192,1536]{2,1,0:T(8,128)(2,1)}, u32[]{:S(2)}, u32[]{:S(2)}) collective-permute-start(bf16[2,192,1536]{2,1,0:T(8,128)(2,1)} %pad_maximum_fusion.9), channel_id=1, source_target_pairs={{0,8},{4,12},{8,16},{12,20},{16,24},{20,28},{24,0},{28,4},{1,9},{5... | collective-permute-start | bytes 3538952 | tf_op jit(solution)/shard_map/ppermute | solution.py:386
  76.2 34.9 %collective-permute-start.6 = (bf16[4,197,768]{2,0,1:T(4,128)(2,1)}, bf16[4,197,768]{2,0,1:T(4,128)(2,1)}, u32[]{:S(2)}, u32[]{:S(2)}) collective-permute-start(bf16[4,197,768]{2,0,1:T(4,128)(2,1)} %copy.279), channel_id=1, source_target_pairs={{0,2},{2,0},{1,3},{3,1},{4,6},{6,4},{5,7},{7,5},{8,10},{10,8},{9,1... | collective-permute-start | bytes 3631112 | tf_op jit(solution)/shard_map/ppermute | solution.py:380
  78.8 32.1 %collective-permute-start.15 = (bf16[2,192,1536]{2,1,0:T(8,128)(2,1)}, bf16[2,192,1536]{2,1,0:T(8,128)(2,1)}, u32[]{:S(2)}, u32[]{:S(2)}) collective-permute-start(bf16[2,192,1536]{2,1,0:T(8,128)(2,1)} %pad_maximum_fusion.8), channel_id=1, source_target_pairs={{0,8},{4,12},{8,16},{12,20},{16,24},{20,28},{24,0},{28,4},{1,9},{5... | collective-permute-start | bytes 3538952 | tf_op jit(solution)/shard_map/ppermute | solution.py:386
  89.6 35.2 %collective-permute-start.12 = (bf16[788,768]{1,0:T(8,128)(2,1)}, bf16[788,768]{1,0:T(8,128)(2,1)}, u32[]{:S(2)}, u32[]{:S(2)}) collective-permute-start(bf16[788,768]{1,0:T(8,128)(2,1)} %reshape.320), channel_id=1, source_target_pairs={{0,1},{1,0},{2,3},{3,2},{4,5},{5,4},{6,7},{7,6},{8,9},{9,8},{10,11... | collective-permute-start | bytes 3631112 | tf_op jit(solution)/shard_map/ppermute | solution.py:380
  93.3 42.9 %collective-permute-start.20 = (bf16[2,192,1536]{2,1,0:T(8,128)(2,1)}, bf16[2,192,1536]{2,1,0:T(8,128)(2,1)}, u32[]{:S(2)}, u32[]{:S(2)}) collective-permute-start(bf16[2,192,1536]{2,1,0:T(8,128)(2,1)} %collective-permute-done.19), channel_id=1, source_target_pairs={{0,8},{4,12},{8,16},{12,20},{16,24},{20,28},{24,0},{28,4},{1,9},{5... | collective-permute-start | bytes 3538952 | tf_op jit(solution)/shard_map/ppermute | solution.py:386
  110.9 50.6 %collective-permute-start.16 = (bf16[2,192,1536]{2,1,0:T(8,128)(2,1)}, bf16[2,192,1536]{2,1,0:T(8,128)(2,1)}, u32[]{:S(2)}, u32[]{:S(2)}) collective-permute-start(bf16[2,192,1536]{2,1,0:T(8,128)(2,1)} %collective-permute-done.15), channel_id=1, source_target_pairs={{0,8},{4,12},{8,16},{12,20},{16,24},{20,28},{24,0},{28,4},{1,9},{5... | collective-permute-start | bytes 3538952 | tf_op jit(solution)/shard_map/ppermute | solution.py:386
  118.4 48.5 %collective-permute-start.9 = (bf16[788,768]{1,0:T(8,128)(2,1)}, bf16[788,768]{1,0:T(8,128)(2,1)}, u32[]{:S(2)}, u32[]{:S(2)}) collective-permute-start(bf16[788,768]{1,0:T(8,128)(2,1)} %multiply_convert_fusion), channel_id=1, source_target_pairs={{0,1},{1,0},{2,3},{3,2},{4,5},{5,4},{6,7},{7,6},{8,9},{9,8},{10,11... | collective-permute-start | bytes 3631112 | tf_op jit(solution)/shard_map/ppermute | solution.py:380
  129.6 84.5 %collective-permute-start.13 = (bf16[2,788,768]{2,0,1:T(2,128)(2,1)}, bf16[2,788,768]{2,0,1:T(2,128)(2,1)}, u32[]{:S(2)}, u32[]{:S(2)}) collective-permute-start(bf16[2,788,768]{2,0,1:T(2,128)(2,1)} %copy.294), channel_id=1, source_target_pairs={{0,4},{4,0},{8,12},{12,8},{16,20},{20,16},{24,28},{28,24},{1,5},{5... | collective-permute-start | bytes 7262216 | tf_op jit(solution)/shard_map/ppermute | solution.py:389
  136.2 50.6 %collective-permute-start.21 = (bf16[2,192,1536]{2,1,0:T(8,128)(2,1)}, bf16[2,192,1536]{2,1,0:T(8,128)(2,1)}, u32[]{:S(2)}, u32[]{:S(2)}) collective-permute-start(bf16[2,192,1536]{2,1,0:T(8,128)(2,1)} %collective-permute-done.20), channel_id=1, source_target_pairs={{0,8},{4,12},{8,16},{12,20},{16,24},{20,28},{24,0},{28,4},{1,9},{5... | collective-permute-start | bytes 3538952 | tf_op jit(solution)/shard_map/ppermute | solution.py:386
  161.4 50.3 %collective-permute-start.17 = (bf16[2,192,1536]{2,1,0:T(8,128)(2,1)}, bf16[2,192,1536]{2,1,0:T(8,128)(2,1)}, u32[]{:S(2)}, u32[]{:S(2)}) collective-permute-start(bf16[2,192,1536]{2,1,0:T(8,128)(2,1)} %collective-permute-done.16), channel_id=1, source_target_pairs={{0,8},{4,12},{8,16},{12,20},{16,24},{20,28},{24,0},{28,4},{1,9},{5... | collective-permute-start | bytes 3538952 | tf_op jit(solution)/shard_map/ppermute | solution.py:386
  170.3 49.6 %collective-permute-start.10 = (bf16[2,788,768]{2,0,1:T(2,128)(2,1)S(1)}, bf16[2,788,768]{2,0,1:T(2,128)(2,1)S(1)}, u32[]{:S(2)}, u32[]{:S(2)}) collective-permute-start(bf16[2,788,768]{2,0,1:T(2,128)(2,1)S(1)} %copy.288), channel_id=1, source_target_pairs={{0,4},{4,0},{8,12},{12,8},{16,20},{20,16},{24,28},{28,24},{1,5},{5... | collective-permute-start | bytes 7262216 | tf_op jit(solution)/shard_map/ppermute | solution.py:389
  282.3 33.7 %collective-permute-start.40 = (bf16[2,192,1536]{2,1,0:T(8,128)(2,1)}, bf16[2,192,1536]{2,1,0:T(8,128)(2,1)}, u32[]{:S(2)}, u32[]{:S(2)}) collective-permute-start(bf16[2,192,1536]{2,1,0:T(8,128)(2,1)} %dynamic-slice_bitcast_fusion.1), channel_id=1, source_target_pairs={{0,8},{4,12},{8,16},{12,20},{16,24},{20,28},{24,0},{28,4},{1,9},{5... | collective-permute-start | bytes 3538952 | tf_op jit(solution)/shard_map/ppermute | solution.py:386
  296.0 43.0 %collective-permute-start.36 = (bf16[2,192,1536]{2,1,0:T(8,128)(2,1)}, bf16[2,192,1536]{2,1,0:T(8,128)(2,1)}, u32[]{:S(2)}, u32[]{:S(2)}) collective-permute-start(bf16[2,192,1536]{2,1,0:T(8,128)(2,1)} %dynamic-slice_bitcast_fusion.2), channel_id=1, source_target_pairs={{0,8},{4,12},{8,16},{12,20},{16,24},{20,28},{24,0},{28,4},{1,9},{5... | collective-permute-start | bytes 3538952 | tf_op jit(solution)/shard_map/ppermute | solution.py:386
  316.0 74.1 %collective-permute-start.22 = (bf16[2,788,768]{2,0,1:T(2,128)(2,1)S(1)}, bf16[2,788,768]{2,0,1:T(2,128)(2,1)S(1)}, u32[]{:S(2)}, u32[]{:S(2)}) collective-permute-start(bf16[2,788,768]{2,0,1:T(2,128)(2,1)S(1)} %copy.299), channel_id=1, source_target_pairs={{0,4},{4,0},{8,12},{12,8},{16,20},{20,16},{24,28},{28,24},{1,5},{5... | collective-permute-start | bytes 7262216 | tf_op jit(solution)/shard_map/ppermute | solution.py:389
  317.7 46.5 %collective-permute-start.41 = (bf16[2,192,1536]{2,1,0:T(8,128)(2,1)S(1)}, bf16[2,192,1536]{2,1,0:T(8,128)(2,1)S(1)}, u32[]{:S(2)}, u32[]{:S(2)}) collective-permute-start(bf16[2,192,1536]{2,1,0:T(8,128)(2,1)S(1)} %fusion.8), channel_id=1, source_target_pairs={{0,8},{4,12},{8,16},{12,20},{16,24},{20,28},{24,0},{28,4},{1,9},{5... | collective-permute-start | bytes 3538952 | tf_op jit(solution)/shard_map/ppermute | solution.py:386
  340.8 48.7 %collective-permute-start.37 = (bf16[2,192,1536]{2,1,0:T(8,128)(2,1)S(1)}, bf16[2,192,1536]{2,1,0:T(8,128)(2,1)S(1)}, u32[]{:S(2)}, u32[]{:S(2)}) collective-permute-start(bf16[2,192,1536]{2,1,0:T(8,128)(2,1)S(1)} %fusion.10), channel_id=1, source_target_pairs={{0,8},{4,12},{8,16},{12,20},{16,24},{20,28},{24,0},{28,4},{1,9},{5... | collective-permute-start | bytes 3538952 | tf_op jit(solution)/shard_map/ppermute | solution.py:386
  364.5 50.3 %collective-permute-start.42 = (bf16[2,192,1536]{2,1,0:T(8,128)(2,1)S(1)}, bf16[2,192,1536]{2,1,0:T(8,128)(2,1)S(1)}, u32[]{:S(2)}, u32[]{:S(2)}) collective-permute-start(bf16[2,192,1536]{2,1,0:T(8,128)(2,1)S(1)} %fusion.7), channel_id=1, source_target_pairs={{0,8},{4,12},{8,16},{12,20},{16,24},{20,28},{24,0},{28,4},{1,9},{5... | collective-permute-start | bytes 3538952 | tf_op jit(solution)/shard_map/ppermute | solution.py:386
  389.8 49.1 %collective-permute-start.38 = (bf16[2,192,1536]{2,1,0:T(8,128)(2,1)S(1)}, bf16[2,192,1536]{2,1,0:T(8,128)(2,1)S(1)}, u32[]{:S(2)}, u32[]{:S(2)}) collective-permute-start(bf16[2,192,1536]{2,1,0:T(8,128)(2,1)S(1)} %fusion.9), channel_id=1, source_target_pairs={{0,8},{4,12},{8,16},{12,20},{16,24},{20,28},{24,0},{28,4},{1,9},{5... | collective-permute-start | bytes 3538952 | tf_op jit(solution)/shard_map/ppermute | solution.py:386
  390.6 49.6 %collective-permute-start.23 = (bf16[788,768]{1,0:T(8,128)(2,1)S(1)}, bf16[788,768]{1,0:T(8,128)(2,1)S(1)}, u32[]{:S(2)}, u32[]{:S(2)}) collective-permute-start(bf16[788,768]{1,0:T(8,128)(2,1)S(1)} %fusion.14), channel_id=1, source_target_pairs={{0,1},{1,0},{2,3},{3,2},{4,5},{5,4},{6,7},{7,6},{8,9},{9,8},{10,11... | collective-permute-start | bytes 3631112 | tf_op jit(solution)/shard_map/ppermute | solution.py:380
  554.5 35.8 %collective-permute-start.26 = (bf16[788,768]{1,0:T(8,128)(2,1)}, bf16[788,768]{1,0:T(8,128)(2,1)}, u32[]{:S(2)}, u32[]{:S(2)}) collective-permute-start(bf16[788,768]{1,0:T(8,128)(2,1)} %fusion.15), channel_id=1, source_target_pairs={{0,1},{1,0},{2,3},{3,2},{4,5},{5,4},{6,7},{7,6},{8,9},{9,8},{10,11... | collective-permute-start | bytes 3631112 | tf_op jit(solution)/shard_map/ppermute | solution.py:380
  (74 other events, 956.7 us)

commit v2 on v1

v2 whole, which is shorter than its diff:
```python
import functools

import jax
import jax.numpy as jnp
from jax import lax
from jax.experimental import pallas as pl
from jax.experimental.pallas import tpu as pltpu
from jax.sharding import PartitionSpec as P

HEAD_DIM = 64
CORES = 2
EPS = 1e-06
LOW = -1e30
F32 = jnp.float32
BF16 = jnp.bfloat16
VMEM_LIMIT = 56 * 1024 * 1024


def dot(a, b, ca, cb):
    return lax.dot_general(a, b, (((ca,), (cb,)), ((), ())), preferred_element_type=F32)


def shaped(shape, kind):
    return jax.ShapeDtypeStruct(shape, kind)


def params(dims=1):
    return pltpu.CompilerParams(
        dimension_semantics=("arbitrary",) * dims, vmem_limit_bytes=VMEM_LIMIT
    )


def cost(flops, size, powers=0):
    return pl.CostEstimate(flops=flops, bytes_accessed=size, transcendentals=powers)


def after(value, *others):
    return lax.optimization_barrier((value,) + others)[0]


def norm_parts(rows):
    average = jnp.mean(rows, axis=-1, keepdims=True)
    centred = rows - average
    spread = jnp.mean(centred * centred, axis=-1, keepdims=True)
    scale = lax.rsqrt(spread + EPS)
    return centred * scale, scale


def softmax_rows(q, own_k, real):
    scores = jnp.where(real, dot(q, own_k, 1, 1) * (HEAD_DIM**-0.5), LOW)
    powers = jnp.exp(scores - jnp.max(scores, axis=-1, keepdims=True))
    return powers / jnp.sum(powers, axis=-1, keepdims=True)


def attend_kernel(seq, x_ref, gain_ref, wqkv_ref, wo_ref, part_ref, qkv_ref, ctx_ref):
    width = wo_ref.shape[1]
    span = x_ref.shape[0]
    unit, _ = norm_parts(x_ref[...].astype(F32))
    normed = (unit * gain_ref[...]).astype(BF16)
    for part in range(3):
        cols = slice(part * width, (part + 1) * width)
        qkv_ref[:, cols] = dot(normed, wqkv_ref[:, cols], 1, 0).astype(BF16)
    lane = lax.broadcasted_iota(jnp.int32, (span, 128), 1)
    real = lax.broadcasted_iota(jnp.int32, (span, span), 1) < seq
    for pair in range(width // 128):
        q, k, v = (
            qkv_ref[:, part * width + pair * 128 : part * width + (pair + 1) * 128]
            for part in range(3)
        )
        ctx = jnp.zeros((span, 128), F32)
        for side in range(2):
            mine = (lane >= 64) if side else (lane < 64)
            own_k = jnp.where(mine, k, jnp.zeros_like(k))
            own_v = jnp.where(mine, v, jnp.zeros_like(v))
            weights = softmax_rows(q, own_k, real)
            ctx = ctx + dot(weights.astype(BF16), own_v, 1, 0)
        ctx_ref[:, pair * 128 : (pair + 1) * 128] = ctx.astype(BF16)
    part_ref[...] = dot(ctx_ref[...], wo_ref[...], 1, 1).astype(BF16)


def attend(inputs, gain, packed, width, images, seq):
    rows, model = inputs.shape
    span = rows // images
    image = lambda last: pl.BlockSpec((span, last), lambda i: (i, 0))
    return pl.pallas_call(
        functools.partial(attend_kernel, seq),
        grid=(images,),
        in_specs=[
            image(model),
            pl.BlockSpec((1, model), lambda i: (0, 0)),
            pl.BlockSpec((model, 3 * width), lambda i: (0, 0)),
            pl.BlockSpec((model, width), lambda i: (0, 3)),
        ],
        out_specs=[image(model), image(3 * width), image(width)],
        out_shape=[
            shaped((rows, model), BF16), shaped((rows, 3 * width), BF16), shaped((rows, width), BF16)
        ],
        compiler_params=params(),
        cost_estimate=cost(10 * rows * model * width, 8 * rows * model, rows * span * width // 64),
        name="attend",
    )(inputs, gain, packed, packed)


def attend_back_kernel(
    seq, gain_at,
    x_ref, gain_ref, datt_ref, qkv_ref, ctx_ref, wqkv_ref, wo_ref, side_ref,
    dnorm_ref, stats_ref, pack_ref, dproj_ref, dgain_ref, dwqkv_ref, dwo_ref,
):
    width = wo_ref.shape[1]
    span, model = x_ref.shape
    step = pl.program_id(0)

    @pl.when(step == 0)
    def _():
        dgain_ref[...] = jnp.zeros_like(dgain_ref)
        dwqkv_ref[...] = jnp.zeros_like(dwqkv_ref)
        dwo_ref[...] = jnp.zeros_like(dwo_ref)

    datt = datt_ref[...]
    dwo_ref[...] += dot(datt, ctx_ref[...], 0, 0)
    dctx_all = dot(datt, wo_ref[...], 1, 0).astype(BF16)
    lane = lax.broadcasted_iota(jnp.int32, (span, 128), 1)
    real = lax.broadcasted_iota(jnp.int32, (span, span), 1) < seq
    for pair in range(width // 128):
        q, k, v = (
            qkv_ref[:, part * width + pair * 128 : part * width + (pair + 1) * 128]
            for part in range(3)
        )
        dctx = dctx_all[:, pair * 128 : (pair + 1) * 128]
        dq = jnp.zeros((span, 128), F32)
        dk = jnp.zeros((span, 128), F32)
        dv = jnp.zeros((span, 128), F32)
        for side in range(2):
            mine = (lane >= 64) if side else (lane < 64)
            own = lambda t: jnp.where(mine, t, jnp.zeros_like(t))
            own_k, own_v = own(k), own(v)
            weights = softmax_rows(q, own_k, real)
            dweights = dot(dctx, own_v, 1, 1)
            inner = jnp.sum(dweights * weights, axis=-1, keepdims=True)
            dscores = (weights * (dweights - inner)).astype(BF16)
            dq = dq + dot(dscores, own_k, 1, 0)
            dk = dk + dot(dscores, own(q), 0, 0)
            dv = dv + dot(weights.astype(BF16), own(dctx), 0, 0)
        for part, value in enumerate((dq * HEAD_DIM**-0.5, dk * HEAD_DIM**-0.5, dv)):
            start = part * width + pair * 128
            dproj_ref[:, start : start + 128] = value.astype(BF16)
    dproj = dproj_ref[...]
    gain = gain_ref[...]
    unit, _ = norm_parts(x_ref[...].astype(F32))
    normed = (unit * gain).astype(BF16)
    dwqkv_ref[...] += dot(normed, dproj, 0, 0)
    dnormed = dot(dproj, wqkv_ref[...], 1, 1)
    halves, _, half = dnorm_ref.shape
    for h in range(halves):
        dnorm_ref[h] = dnormed[:, h * half : (h + 1) * half].astype(BF16)
    along = dnormed * unit
    dgain_ref[...] += jnp.sum(along, axis=0, keepdims=True)
    first = jnp.sum(dnormed * gain, axis=-1, keepdims=True)
    second = jnp.sum(along * gain, axis=-1, keepdims=True)
    stats_ref[...] = jnp.where(lane == 0, first, jnp.where(lane == 1, second, 0.0))

    @pl.when(step == pl.num_programs(0) - 1)
    def _():
        pack_ref[:, : 3 * width] = dwqkv_ref[...].astype(BF16)
        pack_ref[:, 3 * width : 4 * width] = dwo_ref[...].astype(BF16)
        line = lax.broadcasted_iota(jnp.int32, (128, model), 0)
        column = jnp.where(line == gain_at, dgain_ref[...], 0.0).T
        pack_ref[:, 4 * width :] = (side_ref[...] + column).astype(BF16)


def attend_back(inputs, gain, datt, qkv, ctx, packed, dside, gain_at, width, images, seq, halves):
    rows, model = inputs.shape
    span = rows // images
    image = lambda last: pl.BlockSpec((span, last), lambda i: (i, 0))
    fixed = lambda *size: pl.BlockSpec(size, lambda i: (0, 0))
    return pl.pallas_call(
        functools.partial(attend_back_kernel, seq, gain_at),
        grid=(images,),
        in_specs=[
            image(model), fixed(1, model), image(model), image(3 * width), image(width),
            fixed(model, 3 * width), pl.BlockSpec((model, width), lambda i: (0, 3)),
            fixed(model, 128),
        ],
        out_specs=[
            pl.BlockSpec((halves, span, model // halves), lambda i: (0, i, 0)),
            image(128),
            fixed(*packed.shape),
        ],
        out_shape=[
            shaped((halves, rows, model // halves), BF16),
            shaped((rows, 128), F32),
            shaped(packed.shape, BF16),
        ],
        scratch_shapes=[
            pltpu.VMEM((span, 3 * width), BF16),
            pltpu.VMEM((1, model), F32),
            pltpu.VMEM((model, 3 * width), F32),
            pltpu.VMEM((model, width), F32),
        ],
        compiler_params=params(),
        cost_estimate=cost(28 * rows * model * width, 12 * rows * model, rows * span * width // 64),
        name="attend_back",
    )(inputs, gain, datt, qkv, ctx, packed, packed, dside)


def expert_kernel(depth, blocks, place_ref, slot_ref, router_ref, *refs):
    x_refs, refs = refs[:blocks], refs[blocks:]
    grad_refs, refs = refs[:blocks], refs[blocks:]
    win_refs, refs = refs[:depth], refs[depth:]
    wout_refs, refs = refs[:depth], refs[depth:]
    (
        rows_ref, grows_ref, gact_ref, dhid_ref, dchosen_ref, drows_ref, yrows_ref, probs_ref,
        win_all, wout_all,
    ) = refs
    _, slots, model = rows_ref.shape
    tokens = x_refs[0].shape[0]
    part_rows, width = win_refs[0].shape[-2:]
    step = pl.program_id(0)

    @pl.when(step == 0)
    def _():
        for k in range(depth):
            owner = lax.rem(place_ref[0] - k + depth, depth)
            at = pl.ds(pl.multiple_of(owner * part_rows, 16), part_rows)
            win_all[at, :] = win_refs[k][...]
            wout_all[at, :] = wout_refs[k][0]

    mask = lax.broadcasted_iota(jnp.int32, (slots, tokens), 0) == slot_ref[0]
    pick = jnp.where(mask, 1.0, 0.0).astype(BF16)
    for b in range(blocks):

        @pl.when(step == b)
        def _(b=b):
            rows_ref[0] = dot(pick, x_refs[b][...], 1, 0).astype(BF16)
            grows_ref[0] = dot(pick, grad_refs[b][...], 1, 0).astype(BF16)
            logits = dot(router_ref[...], x_refs[b][...], 1, 1)
            powers = jnp.exp(logits - jnp.max(logits, axis=0, keepdims=True))
            probs_ref[0] = powers / jnp.sum(powers, axis=0, keepdims=True)

    probs = probs_ref[0]
    line = lax.broadcasted_iota(jnp.int32, probs.shape, 0)
    own = jnp.sum(jnp.where(line == place_ref[1], probs, 0.0), axis=0, keepdims=True)
    gate = jnp.sum(jnp.where(mask, own, 0.0), axis=1, keepdims=True)
    rows, grows = rows_ref[0], grows_ref[0]
    dgate = jnp.zeros((slots, 1), F32)
    drows = jnp.zeros((slots, model), F32)
    yrows = jnp.zeros((slots, model), F32)
    tile = 512 if width % 512 == 0 else width
    curve = 0.7978845608028654
    for start in range(0, width, tile):
        cols = slice(start, start + tile)
        win, wout = win_all[:, cols], wout_all[:, cols]
        hidden = dot(rows, win, 1, 0)
        pulled = dot(grows, wout, 1, 0)
        square = hidden * hidden
        bend = jnp.tanh(hidden * (curve + curve * 0.044715 * square))
        half = 0.5 + 0.5 * bend
        active = hidden * half
        slope = half + 0.5 * hidden * (1.0 - bend * bend) * (
            curve + 3.0 * curve * 0.044715 * square
        )
        dgate = dgate + jnp.sum(active * pulled, axis=1, keepdims=True)
        gact = (gate * active).astype(BF16)
        dhid = (gate * pulled * slope).astype(BF16)
        gact_ref[0, :, cols] = gact
        dhid_ref[0, :, cols] = dhid
        drows = drows + dot(dhid, win, 1, 1)
        yrows = yrows + dot(gact, wout, 1, 1)
    dchosen_ref[0] = jnp.sum(jnp.where(mask, dgate, 0.0), axis=0, keepdims=True)
    drows_ref[0] = drows.astype(BF16)
    yrows_ref[0] = yrows.astype(BF16)


def run_expert(index, place, slot_of, router_rows, xs, grads, w_in, w_out, slots):
    blocks, depth = len(xs), len(w_in)
    tokens, model = xs[0].shape
    part_rows, width = w_in[0].shape
    experts = router_rows.shape[0]
    fixed = lambda *size: pl.BlockSpec(
        size, lambda b, s: (0,) * len(size), pipeline_mode=pl.Buffered(1)
    )
    block = lambda *size: pl.BlockSpec((1,) + size, lambda b, s: (b, 0, 0))
    return pl.pallas_call(
        functools.partial(expert_kernel, depth, blocks),
        grid_spec=pltpu.PrefetchScalarGridSpec(
            num_scalar_prefetch=1,
            grid=(blocks,),
            in_specs=[block(1, tokens), fixed(experts, model)]
            + [fixed(tokens, model)] * (2 * blocks)
            + [fixed(part_rows, width)] * depth
            + [
                pl.BlockSpec(
                    (1, part_rows, width), lambda b, s: (index, 0, 0),
                    pipeline_mode=pl.Buffered(1),
                )
            ]
            * depth,
            out_specs=[
                block(slots, model), block(slots, model), block(slots, width), block(slots, width),
                block(1, tokens), block(slots, model), block(slots, model), block(experts, tokens),
            ],
            scratch_shapes=[pltpu.VMEM((model, width), BF16)] * 2,
        ),
        out_shape=[
            shaped((blocks, slots, model), BF16), shaped((blocks, slots, model), BF16),
            shaped((blocks, slots, width), BF16), shaped((blocks, slots, width), BF16),
            shaped((blocks, 1, tokens), F32), shaped((blocks, slots, model), BF16),
            shaped((blocks, slots, model), BF16), shaped((blocks, experts, tokens), F32),
        ],
        compiler_params=params(),
        cost_estimate=cost(
            8 * blocks * slots * model * width + 4 * blocks * slots * model * tokens,
            16 * blocks * slots * model,
            blocks * slots * width,
        ),
        name="expert",
    )(place, slot_of, router_rows, *xs, *grads, *w_in, *w_out)


def weight_grad_kernel(depth, place_ref, rows_ref, cols_ref, *refs):
    out_refs, total_ref = refs[:depth], refs[depth]
    blocks, slots, model = rows_ref.shape
    tile = cols_ref.shape[2]
    part_rows = model // depth
    left = rows_ref[...].reshape(blocks * slots, model)
    right = cols_ref[...].reshape(blocks * slots, tile)
    total_ref[...] = dot(left, right, 0, 0)
    for k in range(depth):
        owner = lax.rem(place_ref[0] - k + depth, depth)
        at = pl.ds(pl.multiple_of(owner * part_rows, 16), part_rows)
        out_refs[k][...] = total_ref[at, :].astype(BF16)


def weight_grad(place, rows, cols, depth):
    blocks, slots, model = rows.shape
    width = cols.shape[2]
    tile = width // 2 if width % 256 == 0 else width
    return pl.pallas_call(
        functools.partial(weight_grad_kernel, depth),
        grid_spec=pltpu.PrefetchScalarGridSpec(
            num_scalar_prefetch=1,
            grid=(width // tile,),
            in_specs=[
                pl.BlockSpec((blocks, slots, model), lambda f, s: (0, 0, 0)),
                pl.BlockSpec((blocks, slots, tile), lambda f, s: (0, 0, f)),
            ],
            out_specs=[pl.BlockSpec((model // depth, tile), lambda f, s: (0, f))] * depth,
            scratch_shapes=[pltpu.VMEM((model, tile), F32)],
        ),
        out_shape=[shaped((model // depth, width), BF16)] * depth,
        compiler_params=params(),
        cost_estimate=cost(
            2 * blocks * slots * model * width,
            2 * (blocks * slots * (model + width) + model * width),
        ),
        name="weight_grad",
    )(place, rows, cols)


def combine_kernel(local, added, slot_ref, *refs):
    rows_refs, refs = refs[:local], refs[local:]
    out_ref = refs[-1]
    tokens = out_ref.shape[-2]
    slots, model = rows_refs[0].shape[1:]
    at = lax.broadcasted_iota(jnp.int32, (tokens, slots), 1)
    total = refs[0][...].astype(F32) if added else jnp.zeros((tokens, model), F32)
    for e in range(local):
        pick = jnp.where(at == slot_ref[0, :, e : e + 1], 1.0, 0.0).astype(BF16)
        total = total + dot(pick, rows_refs[e][0], 1, 0)
    out_ref[...] = total.astype(BF16)


def combine(slot_cols, rows, b, add=None):
    _, tokens, local = slot_cols.shape
    slots, model = rows[0].shape[1:]
    whole = pl.BlockSpec((tokens, model), lambda i: (0, 0))
    return pl.pallas_call(
        functools.partial(combine_kernel, local, add is not None),
        grid=(1,),
        in_specs=[pl.BlockSpec((1, tokens, local), lambda i: (b, 0, 0))]
        + [pl.BlockSpec((1, slots, model), lambda i: (b, 0, 0))] * local
        + [whole] * (add is not None),
        out_specs=whole,
        out_shape=shaped((tokens, model), BF16),
        compiler_params=params(),
        cost_estimate=cost(
            2 * local * slots * model * tokens, 2 * model * (local * slots + 2 * tokens)
        ),
        name="combine",
    )(slot_cols, *rows, *(() if add is None else (add,)))


def combine_back_kernel(local, added, place_ref, slot_ref, *refs):
    rows_refs, refs = refs[:local], refs[local:]
    dchosen_refs, refs = refs[:local], refs[local:]
    probs_ref, router_ref, x_ref = refs[:3]
    out_ref, drouter_ref = refs[-2:]
    tokens = out_ref.shape[0]
    slots = rows_refs[0].shape[1]
    at = lax.broadcasted_iota(jnp.int32, (tokens, slots), 1)
    probs = probs_ref[0]
    line = lax.broadcasted_iota(jnp.int32, probs.shape, 0)
    dprobs = jnp.zeros_like(probs)
    for e in range(local):
        dprobs = jnp.where(line == place_ref[1] + e, dchosen_refs[e][0], dprobs)
    inner = jnp.sum(dprobs * probs, axis=0, keepdims=True)
    dlogits = (probs * (dprobs - inner)).astype(BF16)
    drouter_ref[...] = dot(dlogits, x_ref[...], 1, 0)
    total = dot(dlogits, router_ref[...], 0, 0)
    if added:
        total = total + refs[3][...].astype(F32)
    for e in range(local):
        pick = jnp.where(at == slot_ref[0, :, e : e + 1], 1.0, 0.0).astype(BF16)
        total = total + dot(pick, rows_refs[e][0], 1, 0)
    out_ref[...] = total.astype(BF16)


def combine_back(place, slot_cols, rows, dchosen, probs, router_rows, x, b, add=None):
    _, tokens, local = slot_cols.shape
    slots, model = rows[0].shape[1:]
    experts = router_rows.shape[0]
    whole = pl.BlockSpec((tokens, model), lambda i, s: (0, 0))
    block = lambda *size: pl.BlockSpec((1,) + size, lambda i, s: (b, 0, 0))
    small = pl.BlockSpec((experts, model), lambda i, s: (0, 0))
    return pl.pallas_call(
        functools.partial(combine_back_kernel, local, add is not None),
        grid_spec=pltpu.PrefetchScalarGridSpec(
            num_scalar_prefetch=1,
            grid=(1,),
            in_specs=[block(tokens, local)]
            + [block(slots, model)] * local
            + [block(1, tokens)] * local
            + [block(experts, tokens), small, whole]
            + [whole] * (add is not None),
            out_specs=[whole, small],
        ),
        out_shape=[shaped((tokens, model), BF16), shaped((experts, model), F32)],
        compiler_params=params(),
        cost_estimate=cost(
            2 * local * slots * model * tokens, 2 * model * (local * slots + 3 * tokens)
        ),
        name="combine_back",
    )(place, slot_cols, *rows, *dchosen, probs, router_rows, x, *(() if add is None else (add,)))


def per_device(
    block_in, cotangent, route_ids, gain_attn, w_qkv, w_out_attn, gain_moe, router, w_in, w_out
):
    n_dp, n_heads, n_exp = (lax.axis_size(name) for name in ("dp", "heads", "expert"))
    n_z = n_dp // CORES
    dp, head, exp = (lax.axis_index(name) for name in ("dp", "heads", "expert"))
    z, core = dp // CORES, dp % CORES
    low = core == 0
    images, seq, half_width = block_in.shape
    span = -(-seq // 16) * 16
    rows = images * span
    model = half_width * n_heads
    width = w_qkv.shape[2]
    shard = w_qkv.shape[0]
    expert_count = router.shape[1]
    group = w_in.shape[1]
    local = group // CORES
    part_rows, _, hidden_width = w_in.shape
    capacity = 20 * images * seq // (7 * expert_count)
    slots = -(-capacity // 16) * 16
    blocks = n_exp * CORES
    rest = 128

    def shift(value, axis, step):
        size = lax.axis_size(axis)
        return lax.ppermute(value, axis, [(i, (i + step) % size) for i in range(size)])

    def shift_z(value, step):
        pairs = [
            (a * CORES + c, ((a + step) % n_z) * CORES + c) for a in range(n_z) for c in range(CORES)
        ]
        return lax.ppermute(value, "dp", pairs)

    def swap_core(value):
        return lax.ppermute(value, "dp", [(i, i ^ 1) for i in range(n_dp)])

    def place_at(pieces, index, count):
        if count == 2:
            first = index == 0
            return jnp.stack(
                [jnp.where(first, pieces[0], pieces[1]), jnp.where(first, pieces[1], pieces[0])]
            )
        out = jnp.zeros((count,) + pieces[0].shape, pieces[0].dtype)
        for k, piece in enumerate(pieces):
            out = lax.dynamic_update_index_in_dim(out, piece, (index - k) % count, 0)
        return out

    def spread(value, axis):
        return [value] + [shift(value, axis, k) for k in range(1, lax.axis_size(axis))]

    def take(value, index, dim=0):
        return lax.dynamic_index_in_dim(value, index, dim, keepdims=False)

    tail = jnp.concatenate(
        [router, gain_attn[:, None], gain_moe[:, None],
         jnp.zeros((shard, rest - expert_count - 2), BF16)], axis=1
    )
    own_pack = jnp.concatenate([w_qkv.reshape(shard, 3 * width), w_out_attn, tail], axis=1)
    columns = own_pack.shape[1]
    pack_z = place_at([own_pack] + [shift_z(own_pack, k) for k in range(1, n_z)], z, n_z)
    pack = place_at(spread(pack_z, "expert"), exp, n_exp)
    other_pack = swap_core(pack)
    pack = jnp.stack([jnp.where(low, pack, other_pack), jnp.where(low, other_pack, pack)])
    pack = pack.transpose(2, 0, 1, 3, 4).reshape(model, columns)
    side = pack[:, 4 * width :].T
    router_rows = side[:expert_count]
    gain_one = side[expert_count : expert_count + 1].astype(F32)
    gain_two = side[expert_count + 1 : expert_count + 2].astype(F32)

    def full_rows(value):
        padded = jnp.pad(value, ((0, 0), (0, span - seq), (0, 0))).reshape(rows, half_width)
        parts = place_at(spread(padded, "heads"), head, n_heads)
        return jnp.concatenate([parts[i] for i in range(n_heads)], axis=-1)

    inputs = full_rows(block_in)

    def expert_shards(weight):
        by_core = weight.reshape(part_rows, CORES, local, hidden_width).transpose(1, 2, 0, 3)
        other = swap_core(take(by_core, 1 - core))
        mine = take(by_core, core)
        return jnp.concatenate(
            [jnp.where(low, mine, other), jnp.where(low, other, mine)], axis=1
        )

    def ring(piece):
        pieces = [piece]
        for _ in range(1, n_z):
            pieces.append(shift_z(pieces[-1], 1))
        return pieces

    out_pieces = ring(expert_shards(w_out))
    in_shards = expert_shards(w_in)
    in_pieces = []
    for e in range(local):
        hold = pack_z if e == 0 else out_pieces[1]
        in_pieces.append(ring(after(in_shards[e], hold)))

    def blocks_of(value, hold=()):
        along = spread(value, "expert")
        along = along[:1] + [after(part, *hold) for part in along[1:]]
        return along + [swap_core(part) for part in along]

    ids = jnp.pad(route_ids, ((0, 0), (0, span - seq), (0, 0)), constant_values=-1)
    ids_all = jnp.stack(blocks_of(ids.reshape(rows, 2).T))
    first_expert = exp * group + core * local
    named = first_expert + jnp.arange(local, dtype=jnp.int32)
    chosen = jnp.any(ids_all[:, None, :, :] == named[None, :, None, None], axis=2)
    before = (jnp.arange(rows)[:, None] < jnp.arange(rows)[None, :]).astype(BF16)
    rank = jnp.dot(
        chosen.astype(BF16).reshape(blocks * local, rows), before, preferred_element_type=F32
    ).astype(jnp.int32).reshape(blocks, local, rows)
    slot_of = jnp.where(chosen, rank, -1)
    slot_cols = slot_of.transpose(0, 2, 1)
    place = [jnp.stack([z, first_expert + e]).astype(jnp.int32) for e in range(local)]

    inputs_ready = after(inputs, out_pieces[1])
    part, qkv, ctx = attend(inputs_ready, gain_one, pack, width, images, seq)
    grad_full = full_rows(after(cotangent, pack_z))
    grads_all = blocks_of(grad_full)
    part_other = shift(part, "heads", 1)
    for k in range(2, n_heads):
        part_other = part_other + shift(part, "heads", k)
    part_other = after(part_other, out_pieces[min(2, n_z - 1)], in_pieces[0][1])
    middle = inputs.astype(F32) + (part.astype(F32) + part_other.astype(F32))
    unit_two, scale_two = norm_parts(middle)
    normed_two = (unit_two * gain_two).astype(BF16)
    tokens_all = blocks_of(
        normed_two, [pieces[min(2 - e, n_z - 1)] for e, pieces in enumerate(in_pieces[:2])]
    )

    done = []
    moving = []
    mine = []
    for e in range(local):
        shards_in = [p for p in in_pieces[e]]
        if e:
            shards_in[0] = after(shards_in[0], *[m[0] for m in moving])
        result = run_expert(
            e, place[e], slot_of[:, e : e + 1, :], router_rows, tokens_all, grads_all,
            shards_in, out_pieces, slots,
        )
        done.append(result)
        rows_e, grows_e, gact_e, dhid_e = result[:4]
        for left, right in ((grows_e, gact_e), (rows_e, dhid_e)):
            chunks = weight_grad(place[e], left, right, n_z)
            mine.append(chunks)
            moving.append([chunks[1 % n_z]])
    drows, yrows, dchosen = ([r[i] for r in done] for i in (5, 6, 4))
    probs = done[0][7]

    def back_of(b, add=None):
        return combine_back(
            place[0], slot_cols, drows, dchosen, probs, router_rows, tokens_all[b], b, add
        )

    drouter = jnp.zeros((expert_count, model), F32)
    arrived = [None] * n_exp
    for k in reversed(range(n_exp)):
        sent, more = back_of(n_exp + k)
        arrived[k] = swap_core(sent)
        drouter = drouter + more
    from_exp = []
    for k in reversed(range(n_exp)):
        total, more = back_of(k, arrived[k])
        drouter = drouter + more
        if k:
            from_exp.append(shift(total, "expert", -k))
    dsum = total.astype(F32)
    for value in from_exp:
        dsum = dsum + value.astype(F32)
    dsum = dsum.astype(BF16)

    def ring_step(number, hold):
        for r in range(len(moving)):
            came = shift_z(moving[r][-1], 1)
            own = after(mine[r][(number + 1) % n_z], hold)
            total = came.astype(F32) + own.astype(F32)
            moving[r].append(total if number == n_z - 1 else total.astype(BF16))

    ring_step(1, dsum)
    dsum_other = shift(dsum, "heads", 1)
    for k in range(2, n_heads):
        dsum_other = dsum_other + shift(dsum, "heads", k)
    dnormed_two = dsum.astype(F32) + dsum_other.astype(F32)
    scaled = dnormed_two * gain_two
    grad_gain_two = jnp.sum(dnormed_two * unit_two, axis=0)
    dmiddle = grad_full.astype(F32) + scale_two * (
        scaled
        - jnp.mean(scaled, axis=-1, keepdims=True)
        - unit_two * jnp.mean(scaled * unit_two, axis=-1, keepdims=True)
    )
    datt = dmiddle.astype(BF16)
    for number in range(2, n_z - 1):
        ring_step(number, datt)

    dside = jnp.concatenate(
        [drouter, jnp.zeros((1, model), F32), grad_gain_two[None, :],
         jnp.zeros((rest - expert_count - 2, model), F32)], axis=0
    ).T
    dnorm, stats, dpack = attend_back(
        inputs, gain_one, datt, qkv, ctx, pack, dside, expert_count, width, images, seq, n_heads
    )
    if n_z > 2:
        ring_step(n_z - 1, dpack)

    dpack = dpack.reshape(n_z, CORES, n_exp, shard, columns)
    dsent = swap_core(take(dpack, 1 - core, 1))
    dpack = (take(dpack, core, 1).astype(F32) + dsent.astype(F32)).astype(BF16)
    dtotal = take(dpack, exp, 1).astype(F32)
    for k in range(1, n_exp):
        dtotal = dtotal + shift(take(dpack, (exp + k) % n_exp, 1), "expert", k).astype(F32)
    dpack = dtotal.astype(BF16)
    dtotal = take(dpack, z).astype(F32)
    for k in range(1, n_z):
        dtotal = dtotal + shift_z(take(dpack, (z + k) % n_z), k).astype(F32)
    dside = dtotal[:, 4 * width :]
    over_heads = dside[:, : expert_count + 1].T
    summed = over_heads
    for k in range(1, n_heads):
        summed = summed + shift(over_heads, "heads", k)

    def own_half(value):
        return lax.dynamic_slice_in_dim(value, head * half_width, half_width, 1)

    def cut(value):
        return value.astype(BF16).reshape(images, span, half_width)[:, :seq]

    dn_own = take(dnorm, head).astype(F32)
    sums = stats[:, :2].T
    sums_total = sums
    for k in range(1, n_heads):
        dn_own = dn_own + shift(take(dnorm, (head + k) % n_heads), "heads", k).astype(F32)
        sums_total = sums_total + shift(sums, "heads", k)
    unit_one, scale_one = norm_parts(inputs.astype(F32))
    grad_in = own_half(dmiddle) + scale_one * (
        dn_own * own_half(gain_one)
        - sums_total[0][:, None] / model
        - own_half(unit_one) * (sums_total[1][:, None] / model)
    )

    yrows[0] = after(yrows[0], datt)
    y_came = [swap_core(combine(slot_cols, yrows, n_exp + k)) for k in range(n_exp)]
    y_own = combine(slot_cols, yrows, 0, y_came[0]).astype(F32)
    for k in range(1, n_exp):
        y_own = y_own + shift(combine(slot_cols, yrows, k, y_came[k]), "expert", -k).astype(F32)
    y_own = y_own.astype(BF16)
    y_total = own_half(y_own).astype(F32)
    for k in range(1, n_heads):
        there = (head + k) % n_heads
        part_y = lax.dynamic_slice_in_dim(y_own, there * half_width, half_width, 1)
        y_total = y_total + shift(part_y, "heads", k).astype(F32)
    block_out = own_half(middle) + y_total

    def finish(totals):
        stacked = jnp.stack(totals).reshape(local, CORES, part_rows, hidden_width)
        other = swap_core(take(stacked, 1 - core, 1).astype(BF16)).astype(F32)
        own = take(stacked, core, 1).astype(F32)
        joined = jnp.concatenate([jnp.where(low, own, other), jnp.where(low, other, own)], axis=0)
        return joined.transpose(1, 0, 2)

    return (
        cut(block_out),
        cut(grad_in),
        summed[expert_count],
        dtotal[:, : 3 * width].reshape(shard, 3, width),
        dtotal[:, 3 * width : 4 * width],
        dside[:, expert_count + 1],
        summed[:expert_count].T,
        finish([moving[2 * e + 1][-1] for e in range(local)]),
        finish([moving[2 * e][-1] for e in range(local)]),
    )


def solution(mesh):
    return jax.shard_map(
        per_device,
        mesh=mesh,
        in_specs=(
            P(("dp", "expert"), None, "heads"),
            P(("dp", "expert"), None, "heads"),
            P(("dp", "expert"), None, None),
            P(("dp", "expert")),
            P(("dp", "expert"), None, "heads"),
            P(("dp", "expert"), "heads"),
            P(("dp", "expert")),
            P(("dp", "expert"), None),
            P("dp", "expert", "heads"),
            P("dp", "expert", "heads"),
        ),
        out_specs=(
            P(("dp", "expert"), None, "heads"),
            P(("dp", "expert"), None, "heads"),
            P(("dp", "expert")),
            P(("dp", "expert"), None, "heads"),
            P(("dp", "expert"), "heads"),
            P(("dp", "expert")),
            P(("dp", "expert"), None),
            P("dp", "expert", "heads"),
            P("dp", "expert", "heads"),
        ),
        check_vma=False,
    )
```

time: 630 us -> 556 us (0.88)
  local copies, waits for them, and re-layouts: 115 us -> 43.2 us
  Pallas kernels: 112 us -> 158 us
  waiting for transfers between devices: 275 us -> 247 us
  other arithmetic: 72.9 us -> 53.9 us
    ppermute x18 -> x27, waiting for transfers between devices: 220 us -> 161 us  [shift_z(): return lax.ppermute(value, 'dp', pairs)]
    pallas_call x7 -> x16, Pallas kernels: 112 us -> 158 us  [the longest x2 56.8 us: run_expert(): pl.pallas_call(functools.partial(expert_kernel, depth, blocks), grid_spec...]
    ppermute x15, waiting for transfers between devices: 53.5 us -> 85.4 us  [shift(): lax.ppermute(value, axis, [(i, (i + step) % size) for i in range(size)])]
    another operation x9 -> x1, local copies, waits for them, and re-layouts: 19.9 us -> 0.01 us  [per_device(): ids_all = jnp.stack(blocks_of(ids.reshape(rows, 2).T))]
    reshape x16 -> x6, local copies, waits for them, and re-layouts: 20.3 us -> 2.29 us  [the longest x1 0.91 us: per_device(): w_qkv.reshape(shard, 3 * width)]
    dynamic_update_slice x10 -> x4, local copies, waits for them, and re-layouts: 15.3 us -> 1 us  [place_at(): out = lax.dynamic_update_index_in_dim(out, piece, (index - k) % count, 0)]
    ppermute x18 -> x27, starting transfers between devices: 17.9 us -> 27.1 us  [shift_z(): return lax.ppermute(value, 'dp', pairs)]
    concatenate x5 -> x1, other arithmetic: 9.59 us -> 1.1 us  [expert_shards(): jnp.concatenate([jnp.where(low, mine, other), jnp.where(low, other, mine)...]
  transfers between devices with their start and end apart: 44 -> 58, of which waited for: 21 -> 24; matrix products, arithmetic and copies ran while one was open for 24% -> 14% of each run, Pallas kernels for 5% -> 23%
where the time goes in v2:
time: 556 us; the launch traced here: 547 us
  waiting for transfers between devices  247 us (44%)
  Pallas kernels  158 us (28%)
  other arithmetic  53.9 us (10%)
  local copies, waits for them, and re-layouts  43.2 us (8%)
  starting transfers between devices  42.4 us (8%)
    ppermute x27, waiting for transfers between devices, shift_z(): return lax.ppermute(value, 'dp', pairs)  161 us
    ppermute x15, waiting for transfers between devices, shift(): lax.ppermute(value, axis, [(i, (i + step) % size) for i in range(size)])  85.4 us
    pallas_call x2, Pallas kernels, run_expert(): pl.pallas_call(functools.partial(expert_kernel, depth, blocks), grid_spec...  56.8 us
    pallas_call x4, Pallas kernels, weight_grad(): pl.pallas_call(functools.partial(weight_grad_kernel, depth), grid_spec=pl...  30.6 us
    ppermute x27, starting transfers between devices, shift_z(): return lax.ppermute(value, 'dp', pairs)  27.1 us
    unnamed x125, local copies, waits for them, and re-layouts  23 us
    pallas_call x4, Pallas kernels, combine_back(): pl.pallas_call(functools.partial(combine_back_kernel, local, add is not N...  22.6 us
    pallas_call x1, Pallas kernels, attend_back(): pl.pallas_call(functools.partial(attend_back_kernel, seq, gain_at), grid=...  20.4 us
  transfers between devices with their start and end apart: 58, of which 24 were waited for; matrix products, arithmetic and copies ran while one was open for 14% of the time, Pallas kernels for 23%

profile of v2, /device:TPU:0, one launch (start us, length us, event | category | flops | bytes accessed | tf_op | source)
XLA Modules:
  0.0 546.9 jit_solution(2163267631562252818)
XLA Ops:
  12.6 8.5 %collective-permute-done.3 = bf16[48,1664]{1,0:T(8,128)(2,1)} collective-permute-done((bf16[48,1664]{1,0:T(8,128)(2,1)S(1)}, bf16[48,1664]{1,0:T(8,128)(2,1)}, u32[]{:S(2)}, u32[]{:S(2)}) %collective-permute-start.3) | collective-permute-done | bytes 159776 | tf_op jit(solution)/shard_map/ppermute | solution.py:477
  25.1 14.3 %collective-permute-done.6 = bf16[4,48,1664]{2,1,0:T(8,128)(2,1)} collective-permute-done((bf16[4,48,1664]{2,1,0:T(8,128)(2,1)S(1)}, bf16[4,48,1664]{2,1,0:T(8,128)(2,1)}, u32[]{:S(2)}, u32[]{:S(2)}) %collective-permute-start.6) | collective-permute-done | bytes 639008 | tf_op jit(solution)/shard_map/ppermute | solution.py:471
  49.0 13.0 %collective-permute-done = bf16[832,384]{1,0:T(8,128)(2,1)} collective-permute-done((bf16[832,384]{1,0:T(8,128)(2,1)S(1)}, bf16[832,384]{1,0:T(8,128)(2,1)}, u32[]{:S(2)}, u32[]{:S(2)}) %collective-permute-start) | collective-permute-done | bytes 639008 | tf_op jit(solution)/shard_map/ppermute | solution.py:471
  64.4 9.0 %collective-permute-done.2.refs_13_ = bf16[2,192,1536]{2,1,0:T(8,128)(2,1)} collective-permute-done((bf16[2,192,1536]{2,1,0:T(8,128)(2,1)}, bf16[2,192,1536]{2,1,0:T(8,128)(2,1)}, u32[]{:S(2)}, u32[]{:S(2)}) %collective-permute-start.2) | collective-permute-done | bytes 1179680 | tf_op jit(solution)/shard_map/ppermute | solution.py:477
  77.7 10.8 %attend.1 = (bf16[832,768]{1,0:T(8,128)(2,1)}, bf16[832,1152]{1,0:T(8,128)(2,1)}, bf16[832,384]{1,0:T(8,128)(2,1)}) custom-call(bf16[832,768]{1,0:T(8,128)(2,1)} %pad_maximum_fusion.1.x_ref, f32[1,768]{1,0:T(1,128)} %copy.212.gain_ref, bf16[768,1664]{1,0:T(8,128)(2,1)} %bitcast.169, bf16[768,1664]{1,0:T(8,128)(2,1)} %bitcast.170), custom_call_target="tpu_custom_call" | custom-call | flops 2453667840 | bytes 5111808 | tf_op jit(solution)/shard_map/attend/pallas_call | solution.py:85
  98.8 17.0 %collective-permute-done.11.refs_9_ = bf16[192,1536]{1,0:T(8,128)(2,1)} collective-permute-done((bf16[192,1536]{1,0:T(8,128)(2,1)S(1)}, bf16[192,1536]{1,0:T(8,128)(2,1)}, u32[]{:S(2)}, u32[]{:S(2)}) %collective-permute-start.11) | collective-permute-done | bytes 589856 | tf_op jit(solution)/shard_map/ppermute | solution.py:477
  127.8 25.6 %collective-permute-done.12 = s32[2,832]{1,0:T(2,128)S(1)} collective-permute-done((s32[2,832]{1,0:T(2,128)S(1)}, s32[2,832]{1,0:T(2,128)S(1)}, u32[]{:S(2)}, u32[]{:S(2)}) %collective-permute-start.12) | collective-permute-done | bytes 6688 | tf_op jit(solution)/shard_map/ppermute | solution.py:471
  155.2 14.1 %collective-permute-done.17.refs_9_ = bf16[192,1536]{1,0:T(8,128)(2,1)} collective-permute-done((bf16[192,1536]{1,0:T(8,128)(2,1)S(1)}, bf16[192,1536]{1,0:T(8,128)(2,1)}, u32[]{:S(2)}, u32[]{:S(2)}) %collective-permute-start.17) | collective-permute-done | bytes 589856 | tf_op jit(solution)/shard_map/ppermute | solution.py:477
  173.7 13.7 %collective-permute-done.24.refs_11_ = bf16[192,1536]{1,0:T(8,128)(2,1)} collective-permute-done((bf16[192,1536]{1,0:T(8,128)(2,1)S(1)}, bf16[192,1536]{1,0:T(8,128)(2,1)}, u32[]{:S(2)}, u32[]{:S(2)}) %collective-permute-start.24) | collective-permute-done | bytes 589856 | tf_op jit(solution)/shard_map/ppermute | solution.py:477
  192.1 30.0 %collective-permute-done.26.refs_10_ = bf16[192,1536]{1,0:T(8,128)(2,1)} collective-permute-done((bf16[192,1536]{1,0:T(8,128)(2,1)}, bf16[192,1536]{1,0:T(8,128)(2,1)}, u32[]{:S(2)}, u32[]{:S(2)}) %collective-permute-start.26) | collective-permute-done | bytes 589856 | tf_op jit(solution)/shard_map/ppermute | solution.py:477
  222.1 28.1 %expert.2 = (bf16[4,288,768]{2,1,0:T(8,128)(2,1)}, bf16[4,288,768]{2,1,0:T(8,128)(2,1)}, bf16[4,288,1536]{2,1,0:T(8,128)(2,1)}, bf16[4,288,1536]{2,1,0:T(8,128)(...) custom-call(s32[2]{0:T(128)} %pad_add_fusion.1.place_ref, ...), custom_call_target="tpu_custom_call" | custom-call | flops 13816037376 | bytes 14155776 | tf_op jit(solution)/shard_map/expert/pallas_call | solution.py:283
  250.2 7.7 %weight_grad.4 = (bf16[192,1536]{1,0:T(8,128)(2,1)}, bf16[192,1536]{1,0:T(8,128)(2,1)}, bf16[192,1536]{1,0:T(8,128)(2,1)}, bf16[192,1536]{1,0:T(8,128)(2,1)}) custom-call(s32[2]{0:T(128)} %pad_add_fusion.1.place_ref, bf16[4,288,768]{2,1,0:T(8,128)(2,1)} %get-tuple-element.83.rows_ref, bf16[4,288,1536]{2,1,0:T(8,128)(2,1)} %get-tuple-element.84.cols_ref), custom_call_target="tpu_custom_call" | custom-call | flops 2717908992 | bytes 7667712 | tf_op jit(solution)/shard_map/weight_grad/pallas_call | solution.py:338
  257.9 7.7 %weight_grad.5 = (bf16[192,1536]{1,0:T(8,128)(2,1)}, bf16[192,1536]{1,0:T(8,128)(2,1)}, bf16[192,1536]{1,0:T(8,128)(2,1)}, bf16[192,1536]{1,0:T(8,128)(2,1)}) custom-call(s32[2]{0:T(128)} %pad_add_fusion.1.place_ref, bf16[4,288,768]{2,1,0:T(8,128)(2,1)} %get-tuple-element.86.rows_ref, bf16[4,288,1536]{2,1,0:T(8,128)(2,1)} %get-tuple-element.87.cols_ref), custom_call_target="tpu_custom_call" | custom-call | flops 2717908992 | bytes 7667712 | tf_op jit(solution)/shard_map/weight_grad/pallas_call | solution.py:338
  266.4 28.7 %expert.3 = (bf16[4,288,768]{2,1,0:T(8,128)(2,1)}, bf16[4,288,768]{2,1,0:T(8,128)(2,1)}, bf16[4,288,1536]{2,1,0:T(8,128)(2,1)}, bf16[4,288,1536]{2,1,0:T(8,128)(...) custom-call(s32[2]{0:T(128)} %pad_add_fusion.2.place_ref, ...), custom_call_target="tpu_custom_call" | custom-call | flops 13816037376 | bytes 14155776 | tf_op jit(solution)/shard_map/expert/pallas_call | solution.py:283
  317.5 7.6 %weight_grad.6 = (bf16[192,1536]{1,0:T(8,128)(2,1)}, bf16[192,1536]{1,0:T(8,128)(2,1)}, bf16[192,1536]{1,0:T(8,128)(2,1)}, bf16[192,1536]{1,0:T(8,128)(2,1)}) custom-call(s32[2]{0:T(128)} %pad_add_fusion.2.place_ref, bf16[4,288,768]{2,1,0:T(8,128)(2,1)} %get-tuple-element.115.rows_ref, bf16[4,288,1536]{2,1,0:T(8,128)(2,1)} %get-tuple-element.116.cols_ref), custom_call_target="tpu_custom_call" | custom-call | flops 2717908992 | bytes 7667712 | tf_op jit(solution)/shard_map/weight_grad/pallas_call | solution.py:338
  329.4 7.6 %weight_grad.7 = (bf16[192,1536]{1,0:T(8,128)(2,1)}, bf16[192,1536]{1,0:T(8,128)(2,1)}, bf16[192,1536]{1,0:T(8,128)(2,1)}, bf16[192,1536]{1,0:T(8,128)(2,1)}) custom-call(s32[2]{0:T(128)} %pad_add_fusion.2.place_ref, bf16[4,288,768]{2,1,0:T(8,128)(2,1)} %get-tuple-element.130.rows_ref, bf16[4,288,1536]{2,1,0:T(8,128)(2,1)} %get-tuple-element.131.cols_ref), custom_call_target="tpu_custom_call" | custom-call | flops 2717908992 | bytes 7667712 | tf_op jit(solution)/shard_map/weight_grad/pallas_call | solution.py:338
  347.9 12.5 %collective-permute-done.47 = bf16[192,1536]{1,0:T(8,128)(2,1)} collective-permute-done((bf16[192,1536]{1,0:T(8,128)(2,1)}, bf16[192,1536]{1,0:T(8,128)(2,1)}, u32[]{:S(2)}, u32[]{:S(2)}) %collective-permute-start.47) | collective-permute-done | bytes 589856 | tf_op jit(solution)/shard_map/ppermute | solution.py:477
  380.5 20.4 %attend_back.1 = (bf16[2,832,384]{2,1,0:T(8,128)(2,1)}, f32[832,128]{1,0:T(8,128)}, bf16[768,1664]{1,0:T(8,128)(2,1)}) custom-call(bf16[832,768]{1,0:T(8,128)(2,1)} %pad_maximum_fusion.1.x_ref, f32[1,768]{1,0:T(1,128)} %copy.212.gain_ref, bf16[832,768]{1,0:T(8,128)(2,1)} %get-tuple-element.198.datt_ref, bf16[832,1152]{1,0:T(8,128)(2,1)} %get-tuple-element.100.qkv_ref, ...), custom_call_target="tpu_custom_call" | custom-call | flops 6870269952 | bytes 7667712 | tf_op jit(solution)/shard_map/attend_back/pallas_call | solution.py:176
  412.7 10.9 %collective-permute-done.55 = bf16[192,1536]{1,0:T(8,128)(2,1)} collective-permute-done((bf16[192,1536]{1,0:T(8,128)(2,1)}, bf16[192,1536]{1,0:T(8,128)(2,1)}, u32[]{:S(2)}, u32[]{:S(2)}) %collective-permute-start.55) | collective-permute-done | bytes 589856 | tf_op jit(solution)/shard_map/ppermute | solution.py:477
  438.2 10.8 %collective-permute-done.49 = bf16[192,1536]{1,0:T(8,128)(2,1)} collective-permute-done((bf16[192,1536]{1,0:T(8,128)(2,1)}, bf16[192,1536]{1,0:T(8,128)(2,1)}, u32[]{:S(2)}, u32[]{:S(2)}) %collective-permute-start.49) | collective-permute-done | bytes 589856 | tf_op jit(solution)/shard_map/ppermute | solution.py:477
  450.3 11.2 %collective-permute-done.53 = bf16[192,1536]{1,0:T(8,128)(2,1)} collective-permute-done((bf16[192,1536]{1,0:T(8,128)(2,1)S(1)}, bf16[192,1536]{1,0:T(8,128)(2,1)}, u32[]{:S(2)}, u32[]{:S(2)}) %collective-permute-start.53) | collective-permute-done | bytes 589856 | tf_op jit(solution)/shard_map/ppermute | solution.py:477
  462.8 10.4 %collective-permute-done.56 = bf16[192,1536]{1,0:T(8,128)(2,1)} collective-permute-done((bf16[192,1536]{1,0:T(8,128)(2,1)}, bf16[192,1536]{1,0:T(8,128)(2,1)}, u32[]{:S(2)}, u32[]{:S(2)}) %collective-permute-start.56) | collective-permute-done | bytes 589856 | tf_op jit(solution)/shard_map/ppermute | solution.py:477
  488.5 9.0 %collective-permute-done.39 = bf16[4,48,1664]{2,1,0:T(8,128)(2,1)} collective-permute-done((bf16[4,48,1664]{2,1,0:T(8,128)(2,1)S(1)}, bf16[4,48,1664]{2,1,0:T(8,128)(2,1)}, u32[]{:S(2)}, u32[]{:S(2)}) %collective-permute-start.39) | collective-permute-done | bytes 639008 | tf_op jit(solution)/shard_map/ppermute | solution.py:471
  531.1 12.7 %collective-permute-done.35 = bf16[832,384]{1,0:T(8,128)(2,1)} collective-permute-done((bf16[832,384]{1,0:T(8,128)(2,1)S(1)}, bf16[832,384]{1,0:T(8,128)(2,1)}, u32[]{:S(2)}, u32[]{:S(2)}) %collective-permute-start.35) | collective-permute-done | bytes 639008 | tf_op jit(solution)/shard_map/ppermute | solution.py:471
  (344 shorter events, 203.2 us)
Async XLA Ops:
  48.2 41.9 %collective-permute-start.10 = (bf16[2,96,1536]{2,1,0:T(8,128)(2,1)}, bf16[2,96,1536]{2,1,0:T(8,128)(2,1)}, u32[]{:S(2)}, u32[]{:S(2)}) collective-permute-start(bf16[2,96,1536]{2,1,0:T(8,128)(2,1)} %dynamic-slice_bitcast_fusion.3), channel_id=1, source_target_pairs={{0,4},{4,0},{8,12},{12,8},{16,20},{20,16},{24,28},{28,24},{1,5},{5... | collective-permute-start | bytes 1769480 | tf_op jit(solution)/shard_map/ppermute | solution.py:480
  48.4 46.3 %collective-permute-start.20 = (bf16[832,384]{1,0:T(8,128)(2,1)S(1)}, bf16[832,384]{1,0:T(8,128)(2,1)}, u32[]{:S(2)}, u32[]{:S(2)}) collective-permute-start(bf16[832,384]{1,0:T(8,128)(2,1)S(1)} %bitcast.173), channel_id=1, source_target_pairs={{0,2},{2,0},{1,3},{3,1},{4,6},{6,4},{5,7},{7,5},{8,10},{10,8},{9,1... | collective-permute-start | bytes 1916936 | tf_op jit(solution)/shard_map/ppermute | solution.py:471
  73.4 42.4 %collective-permute-start.9 = (bf16[2,192,1536]{2,1,0:T(8,128)(2,1)}, bf16[2,192,1536]{2,1,0:T(8,128)(2,1)}, u32[]{:S(2)}, u32[]{:S(2)}) collective-permute-start(bf16[2,192,1536]{2,1,0:T(8,128)(2,1)} %collective-permute-done.2.refs_13_), channel_id=1, source_target_pairs={{0,8},{4,12},{8,16},{12,20},{16,24},{20,28},{24,0},{28,4},{1,9},{5... | collective-permute-start | bytes 3538952 | tf_op jit(solution)/shard_map/ppermute | solution.py:477
  97.0 57.6 %collective-permute-start.21 = (bf16[832,768]{1,0:T(8,128)(2,1)S(1)}, bf16[832,768]{1,0:T(8,128)(2,1)}, u32[]{:S(2)}, u32[]{:S(2)}) collective-permute-start(bf16[832,768]{1,0:T(8,128)(2,1)S(1)} %pad_maximum_fusion.3.refs_4_), channel_id=1, source_target_pairs={{0,1},{1,0},{2,3},{3,2},{4,5},{5,4},{6,7},{7,6},{8,9},{9,8},{10,11... | collective-permute-start | bytes 3833864 | tf_op jit(solution)/shard_map/ppermute | solution.py:471
  123.5 45.7 %collective-permute-start.15 = (bf16[832,768]{1,0:T(8,128)(2,1)}, bf16[832,768]{1,0:T(8,128)(2,1)}, u32[]{:S(2)}, u32[]{:S(2)}) collective-permute-start(bf16[832,768]{1,0:T(8,128)(2,1)} %multiply_convert_fusion.refs_0_.refs_6_), channel_id=1, source_target_pairs={{0,1},{1,0},{2,3},{3,2},{4,5},{5,4},{6,7},{7,6},{8,9},{9,8},{10,11... | collective-permute-start | bytes 3833864 | tf_op jit(solution)/shard_map/ppermute | solution.py:471
  125.1 45.4 %collective-permute-start.22 = (bf16[832,768]{1,0:T(8,128)(2,1)S(1)}, bf16[832,768]{1,0:T(8,128)(2,1)}, u32[]{:S(2)}, u32[]{:S(2)}) collective-permute-start(bf16[832,768]{1,0:T(8,128)(2,1)S(1)} %pad_maximum_fusion.3.refs_4_), channel_id=1, source_target_pairs={{0,4},{4,0},{8,12},{12,8},{16,20},{20,16},{24,28},{28,24},{1,5},{5... | collective-permute-start | bytes 3833864 | tf_op jit(solution)/shard_map/ppermute | solution.py:480
  169.3 52.8 %collective-permute-start.23 = (bf16[832,768]{1,0:T(8,128)(2,1)}, bf16[832,768]{1,0:T(8,128)(2,1)}, u32[]{:S(2)}, u32[]{:S(2)}) collective-permute-start(bf16[832,768]{1,0:T(8,128)(2,1)} %collective-permute-done.21.refs_5_), channel_id=1, source_target_pairs={{0,4},{4,0},{8,12},{12,8},{16,20},{20,16},{24,28},{28,24},{1,5},{5... | collective-permute-start | bytes 3833864 | tf_op jit(solution)/shard_map/ppermute | solution.py:480
  169.3 52.8 %collective-permute-start.18 = (bf16[832,768]{1,0:T(8,128)(2,1)}, bf16[832,768]{1,0:T(8,128)(2,1)}, u32[]{:S(2)}, u32[]{:S(2)}) collective-permute-start(bf16[832,768]{1,0:T(8,128)(2,1)} %multiply_convert_fusion.refs_0_.refs_6_), channel_id=1, source_target_pairs={{0,4},{4,0},{8,12},{12,8},{16,20},{20,16},{24,28},{28,24},{1,5},{5... | collective-permute-start | bytes 3833864 | tf_op jit(solution)/shard_map/ppermute | solution.py:480
  169.8 52.3 %collective-permute-start.19 = (bf16[832,768]{1,0:T(8,128)(2,1)}, bf16[832,768]{1,0:T(8,128)(2,1)}, u32[]{:S(2)}, u32[]{:S(2)}) collective-permute-start(bf16[832,768]{1,0:T(8,128)(2,1)} %collective-permute-done.15.refs_1_.refs_6_), channel_id=1, source_target_pairs={{0,4},{4,0},{8,12},{12,8},{16,20},{20,16},{24,28},{28,24},{1,5},{5... | collective-permute-start | bytes 3833864 | tf_op jit(solution)/shard_map/ppermute | solution.py:480
  170.5 51.6 %collective-permute-start.25 = (bf16[2,192,1536]{2,1,0:T(8,128)(2,1)}, bf16[2,192,1536]{2,1,0:T(8,128)(2,1)}, u32[]{:S(2)}, u32[]{:S(2)}) collective-permute-start(bf16[2,192,1536]{2,1,0:T(8,128)(2,1)} %collective-permute-done.9.refs_14_), channel_id=1, source_target_pairs={{0,8},{4,12},{8,16},{12,20},{16,24},{20,28},{24,0},{28,4},{1,9},{5... | collective-permute-start | bytes 3538952 | tf_op jit(solution)/shard_map/ppermute | solution.py:477
  222.1 43.5 %collective-permute-start.27 = (bf16[192,1536]{1,0:T(8,128)(2,1)}, bf16[192,1536]{1,0:T(8,128)(2,1)S(1)}, u32[]{:S(2)}, u32[]{:S(2)}) collective-permute-start(bf16[192,1536]{1,0:T(8,128)(2,1)} %collective-permute-done.26.refs_10_), channel_id=1, source_target_pairs={{0,8},{4,12},{8,16},{12,20},{16,24},{20,28},{24,0},{28,4},{1,9},{5... | collective-permute-start | bytes 1769480 | tf_op jit(solution)/shard_map/ppermute | solution.py:477
  316.9 45.6 %collective-permute-start.51 = (bf16[192,1536]{1,0:T(8,128)(2,1)}, bf16[192,1536]{1,0:T(8,128)(2,1)}, u32[]{:S(2)}, u32[]{:S(2)}) collective-permute-start(bf16[192,1536]{1,0:T(8,128)(2,1)} %get-tuple-element.85), channel_id=1, source_target_pairs={{0,8},{4,12},{8,16},{12,20},{16,24},{20,28},{24,0},{28,4},{1,9},{5... | collective-permute-start | bytes 1769480 | tf_op jit(solution)/shard_map/ppermute | solution.py:477
  325.2 35.3 %collective-permute-start.47 = (bf16[192,1536]{1,0:T(8,128)(2,1)}, bf16[192,1536]{1,0:T(8,128)(2,1)}, u32[]{:S(2)}, u32[]{:S(2)}) collective-permute-start(bf16[192,1536]{1,0:T(8,128)(2,1)} %get-tuple-element.117), channel_id=1, source_target_pairs={{0,8},{4,12},{8,16},{12,20},{16,24},{20,28},{24,0},{28,4},{1,9},{5... | collective-permute-start | bytes 1769480 | tf_op jit(solution)/shard_map/ppermute | solution.py:477
  337.1 36.0 %collective-permute-start.54 = (bf16[192,1536]{1,0:T(8,128)(2,1)}, bf16[192,1536]{1,0:T(8,128)(2,1)}, u32[]{:S(2)}, u32[]{:S(2)}) collective-permute-start(bf16[192,1536]{1,0:T(8,128)(2,1)} %get-tuple-element.132), channel_id=1, source_target_pairs={{0,8},{4,12},{8,16},{12,20},{16,24},{20,28},{24,0},{28,4},{1,9},{5... | collective-permute-start | bytes 1769480 | tf_op jit(solution)/shard_map/ppermute | solution.py:477
  347.9 55.3 %collective-permute-start.45 = (bf16[192,1536]{1,0:T(8,128)(2,1)S(1)}, bf16[192,1536]{1,0:T(8,128)(2,1)}, u32[]{:S(2)}, u32[]{:S(2)}) collective-permute-start(bf16[192,1536]{1,0:T(8,128)(2,1)S(1)} %add_convert_fusion.10), channel_id=1, source_target_pairs={{0,8},{4,12},{8,16},{12,20},{16,24},{20,28},{24,0},{28,4},{1,9},{5... | collective-permute-start | bytes 1769480 | tf_op jit(solution)/shard_map/ppermute | solution.py:477
  362.5 43.1 %collective-permute-start.48 = (bf16[192,1536]{1,0:T(8,128)(2,1)}, bf16[192,1536]{1,0:T(8,128)(2,1)}, u32[]{:S(2)}, u32[]{:S(2)}) collective-permute-start(bf16[192,1536]{1,0:T(8,128)(2,1)} %add_convert_fusion.8), channel_id=1, source_target_pairs={{0,8},{4,12},{8,16},{12,20},{16,24},{20,28},{24,0},{28,4},{1,9},{5... | collective-permute-start | bytes 1769480 | tf_op jit(solution)/shard_map/ppermute | solution.py:477
  364.7 46.3 %collective-permute-start.52 = (bf16[192,1536]{1,0:T(8,128)(2,1)}, bf16[192,1536]{1,0:T(8,128)(2,1)}, u32[]{:S(2)}, u32[]{:S(2)}) collective-permute-start(bf16[192,1536]{1,0:T(8,128)(2,1)} %add_convert_fusion.6), channel_id=1, source_target_pairs={{0,8},{4,12},{8,16},{12,20},{16,24},{20,28},{24,0},{28,4},{1,9},{5... | collective-permute-start | bytes 1769480 | tf_op jit(solution)/shard_map/ppermute | solution.py:477
  375.1 48.5 %collective-permute-start.55 = (bf16[192,1536]{1,0:T(8,128)(2,1)}, bf16[192,1536]{1,0:T(8,128)(2,1)}, u32[]{:S(2)}, u32[]{:S(2)}) collective-permute-start(bf16[192,1536]{1,0:T(8,128)(2,1)} %add_convert_fusion.4), channel_id=1, source_target_pairs={{0,8},{4,12},{8,16},{12,20},{16,24},{20,28},{24,0},{28,4},{1,9},{5... | collective-permute-start | bytes 1769480 | tf_op jit(solution)/shard_map/ppermute | solution.py:477
  407.6 41.4 %collective-permute-start.49 = (bf16[192,1536]{1,0:T(8,128)(2,1)}, bf16[192,1536]{1,0:T(8,128)(2,1)}, u32[]{:S(2)}, u32[]{:S(2)}) collective-permute-start(bf16[192,1536]{1,0:T(8,128)(2,1)} %add_convert_fusion.7), channel_id=1, source_target_pairs={{0,8},{4,12},{8,16},{12,20},{16,24},{20,28},{24,0},{28,4},{1,9},{5... | collective-permute-start | bytes 1769480 | tf_op jit(solution)/shard_map/ppermute | solution.py:477
  412.4 49.2 %collective-permute-start.53 = (bf16[192,1536]{1,0:T(8,128)(2,1)S(1)}, bf16[192,1536]{1,0:T(8,128)(2,1)}, u32[]{:S(2)}, u32[]{:S(2)}) collective-permute-start(bf16[192,1536]{1,0:T(8,128)(2,1)S(1)} %add_convert_fusion.5), channel_id=1, source_target_pairs={{0,8},{4,12},{8,16},{12,20},{16,24},{20,28},{24,0},{28,4},{1,9},{5... | collective-permute-start | bytes 1769480 | tf_op jit(solution)/shard_map/ppermute | solution.py:477
  425.7 47.6 %collective-permute-start.56 = (bf16[192,1536]{1,0:T(8,128)(2,1)}, bf16[192,1536]{1,0:T(8,128)(2,1)}, u32[]{:S(2)}, u32[]{:S(2)}) collective-permute-start(bf16[192,1536]{1,0:T(8,128)(2,1)} %add_convert_fusion.3), channel_id=1, source_target_pairs={{0,8},{4,12},{8,16},{12,20},{16,24},{20,28},{24,0},{28,4},{1,9},{5... | collective-permute-start | bytes 1769480 | tf_op jit(solution)/shard_map/ppermute | solution.py:477
  435.1 39.6 %collective-permute-start.36 = (bf16[832,384]{1,0:T(8,128)(2,1)S(1)}, bf16[832,384]{1,0:T(8,128)(2,1)S(1)}, u32[]{:S(2)}, u32[]{:S(2)}) collective-permute-start(bf16[832,384]{1,0:T(8,128)(2,1)S(1)} %dynamic-slice_bitcast_fusion.2), channel_id=1, source_target_pairs={{0,2},{2,0},{1,3},{3,1},{4,6},{6,4},{5,7},{7,5},{8,10},{10,8},{9,1... | collective-permute-start | bytes 1916936 | tf_op jit(solution)/shard_map/ppermute | solution.py:471
  436.7 72.9 %collective-permute-start.32 = (bf16[832,768]{1,0:T(8,128)(2,1)}, bf16[832,768]{1,0:T(8,128)(2,1)}, u32[]{:S(2)}, u32[]{:S(2)}) collective-permute-start(bf16[832,768]{1,0:T(8,128)(2,1)} %combine.4), channel_id=1, source_target_pairs={{0,4},{4,0},{8,12},{12,8},{16,20},{20,16},{24,28},{28,24},{1,5},{5... | collective-permute-start | bytes 3833864 | tf_op jit(solution)/shard_map/ppermute | solution.py:480
  487.0 37.5 %collective-permute-start.34 = (bf16[832,768]{1,0:T(8,128)(2,1)}, bf16[832,768]{1,0:T(8,128)(2,1)}, u32[]{:S(2)}, u32[]{:S(2)}) collective-permute-start(bf16[832,768]{1,0:T(8,128)(2,1)} %combine.7), channel_id=1, source_target_pairs={{0,1},{1,0},{2,3},{3,2},{4,5},{5,4},{6,7},{7,6},{8,9},{9,8},{10,11... | collective-permute-start | bytes 3833864 | tf_op jit(solution)/shard_map/ppermute | solution.py:471
  (91 other events, 1151.1 us)
